TPU v7x, 256 devices: a whole 4x4x8 slice. The times are simulated.
256 devices in a mesh: ctx: 32 (over x, z_hi, core), ch: 8 (over z_lo, y).
Axes of the slice: x: 4, y: 4, z: 8 (z_hi: 4, z_lo: 2; z = z_hi * 2 + z_lo), core: 2. Of those that a mesh axis runs over, the one named last changes fastest.
Arguments:
- query_input: bfloat16 [16384, 4096], P(('ctx', 'ch')), may hold values from -6 to 6
- key_input: bfloat16 [16384, 4096], P(('ctx', 'ch')), may hold values from -6 to 6
- value_input: bfloat16 [16384, 4096], P(('ctx', 'ch')), may hold values from -6 to 6
- filters: bfloat16 [16384, 4096], P('ctx', 'ch'), may hold values from -0.046875 to 0.046875
- direct_gain: float32 [4096], P('ch'), may hold values from -4 to 4
Outputs:
- mixed_output: bfloat16 [16384, 4096], P(('ctx', 'ch'))
All inputs are finite; a program needn't handle non-finite values.
Results may differ from a plain program's by a relative error of at most 0.012.
Values may be sent and summed in bfloat16 or wider, within the bound.
A program may use at most 64 MiB of HBM per device.

v0:
```python
import functools

import jax
import jax.numpy as jnp
import numpy as np
from jax import lax
from jax.experimental import pallas as pl
from jax.experimental.pallas import tpu as pltpu
from jax.sharding import PartitionSpec as P

MESH = pl.DeviceIdType.MESH
SIDE = 128
OCTET = 8
GROUP = 4
X, Z_HI, CORE = 4, 4, 2
Z_LO, Y = 2, 4
OWNERS = X * Z_HI
PEERS = OWNERS * Z_LO
CHUNKS = 2


def tables():
    length = SIDE * SIDE
    side = np.arange(SIDE)
    offset = side + 0.25
    coarse = 2 * np.pi * np.outer(offset, side) / SIDE
    turn = 2 * np.pi * np.outer(offset, side) / length
    fine = 2 * np.pi * np.outer(side, side) / SIDE
    arrival = side.reshape(OWNERS, CORE, Z_LO, 2).transpose(0, 2, 1, 3).reshape(-1)

    def forward(angle):
        return np.concatenate([np.cos(angle), -np.sin(angle)], axis=0)

    angle = coarse[:, arrival].T
    back = np.concatenate([np.cos(angle), -np.sin(angle)], axis=1) / length
    cos, sin = np.cos(fine), np.sin(fine)
    into = np.block([[cos, -sin], [sin, cos]])
    outof = np.block([[cos, sin], [-sin, cos]])
    stacked = [
        np.concatenate([forward(coarse[:, arrival]), forward(coarse)], axis=1),
        into,
        outof,
        back,
        np.concatenate([np.cos(turn), np.sin(turn)], axis=1),
    ]
    return np.concatenate(stacked, axis=0).astype(np.float32)


def halves(table):
    high = table.astype(jnp.bfloat16)
    return high, (table - high.astype(jnp.float32)).astype(jnp.bfloat16)


def dot(left, right):
    return jnp.dot(left, right, preferred_element_type=jnp.float32)


def kernel(
    key_hbm,
    value_hbm,
    filter_hbm,
    gain_ref,
    tables_hbm,
    out_ref,
    key_ref,
    value_ref,
    filter_ref,
    stacked,
    signal_coarse,
    filter_coarse,
    into,
    outof,
    back,
    gated,
    slab,
    signal_turned,
    signal_in,
    filter_turned,
    filter_mid,
    filter_in,
    signal_wide,
    filter_wide,
    spectrum,
    wide,
    sent,
    returned,
    rows,
    load_sems,
    row_send,
    row_recv,
    filter_send,
    filter_recv,
    swap_send,
    swap_recv,
    signal_send,
    signal_recv,
    back_send,
    back_recv,
    out_send,
    out_recv,
):
    count = gated.shape[0]
    ctx = lax.axis_index("ctx")
    ch = lax.axis_index("ch")
    x, z_hi, core = ctx // (Z_HI * CORE), lax.rem(ctx // CORE, Z_HI), lax.rem(ctx, CORE)
    z_lo, y = ch // Y, lax.rem(ch, Y)
    owner = x * Z_HI + z_hi
    me = owner * Z_LO + z_lo
    half = lambda low, other_y, other_core: (low * Y + other_y) * CORE + other_core

    loads = [
        pltpu.make_async_copy(source, target, load_sems.at[n])
        for n, (source, target) in enumerate(
            [
                (filter_hbm, filter_ref),
                (key_hbm, key_ref),
                (value_hbm, value_ref),
                (tables_hbm, stacked),
            ]
        )
    ]
    for load_copy in loads:
        load_copy.start()

    def across(step):
        other = lax.rem(me + step + core * (PEERS - 2 * step), PEERS)
        owner_there, low = other // Z_LO, lax.rem(other, Z_LO)
        return other, owner_there, low, (owner_there * CORE + core, low * Y + y)

    def owners(step):
        other = lax.rem(owner + step + core * (OWNERS - 2 * step), OWNERS)
        return other, (other * CORE + core, ch)

    def aside(step):
        other = lax.rem(y * CORE + core + step, Y * CORE)
        other_y, other_core = other // CORE, lax.rem(other, CORE)
        return other_y, other_core, (owner * CORE + other_core, z_lo * Y + other_y)

    barrier = pltpu.get_barrier_semaphore()

    with jax.named_scope("greet"):

        @pl.loop(1, PEERS)
        def _(step):
            pl.semaphore_signal(barrier, inc=1, device_id=across(step)[-1], device_id_type=MESH)

        @pl.loop(1, Y * CORE)
        def _(step):
            pl.semaphore_signal(barrier, inc=1, device_id=aside(step)[-1], device_id_type=MESH)

    def turned_pair(source, pair, column):
        parts = []
        for tile in (2 * pair, 2 * pair + 1):
            block = source[tile * SIDE : (tile + 1) * SIDE, column * SIDE : (column + 1) * SIDE]
            parts.append(block.astype(jnp.float32).T.reshape(OWNERS, OCTET, SIDE))
        return jnp.concatenate(parts, axis=1).astype(jnp.bfloat16)

    with jax.named_scope("turn_filter"):
        loads[0].wait()
        for column in range(CORE * CHUNKS):
            for pair in range(2):
                filter_turned[:, column, pair * 16 : (pair + 1) * 16, :] = turned_pair(
                    filter_ref, pair, column
                )

    with jax.named_scope("gate"):
        loads[1].wait()
        loads[2].wait()
        gated[...] = (
            key_ref[...].astype(jnp.float32) * value_ref[...].astype(jnp.float32)
        ).astype(jnp.bfloat16)

    with jax.named_scope("await_greet"):
        pl.semaphore_wait(barrier, PEERS + Y * CORE - 2)

    with jax.named_scope("send_filter"):

        @pl.loop(1, OWNERS)
        def _(step):
            other, device = owners(step)
            pltpu.make_async_remote_copy(
                src_ref=filter_turned.at[other],
                dst_ref=filter_mid.at[:, owner],
                send_sem=filter_send,
                recv_sem=filter_recv,
                device_id=device,
                device_id_type=MESH,
            ).start()

        pltpu.make_async_copy(filter_turned.at[owner], filter_mid.at[:, owner], filter_recv).start()

    def columns(low, other_y, other_core, first, size):
        start = half(low, other_y, other_core) * CHUNKS * SIDE + first
        return pl.ds(pl.multiple_of(start, SIDE), size)

    def line_of(other_y, other_core):
        return pl.ds(pl.multiple_of((other_core * Y + other_y) * count, count), count)

    with jax.named_scope("send_rows"):
        span = CHUNKS * SIDE

        @pl.loop(1, Y * CORE)
        def _(step):
            other_y, other_core, device = aside(step)
            for low in range(Z_LO):
                pltpu.make_async_remote_copy(
                    src_ref=gated.at[:, columns(low, other_y, other_core, 0, span)],
                    dst_ref=slab.at[line_of(y, core), pl.ds(low * span, span)],
                    send_sem=row_send,
                    recv_sem=row_recv,
                    device_id=device,
                    device_id_type=MESH,
                ).start()

        for low in range(Z_LO):
            pltpu.make_async_copy(
                gated.at[:, columns(low, y, core, 0, span)],
                slab.at[line_of(y, core), pl.ds(low * span, span)],
                row_recv,
            ).start()

    with jax.named_scope("split_tables"):
        loads[3].wait()
        for target, start in ((signal_coarse, 0), (filter_coarse, SIDE)):
            high, low = halves(stacked[:256, start : start + SIDE])
            target[:, :SIDE], target[:, SIDE:] = high, low
        for target, start in ((into, 256), (outof, 512), (back, 768)):
            target[0], target[1] = halves(stacked[start : start + target.shape[1]])

    with jax.named_scope("await_rows"):
        pltpu.make_async_copy(slab, slab, row_recv).wait()

    with jax.named_scope("send_signal"):
        for chunk in range(CHUNKS):
            for low in range(Z_LO):
                for pair in range(2):
                    signal_turned[
                        chunk, low * OWNERS : (low + 1) * OWNERS, pair * 16 : (pair + 1) * 16, :
                    ] = turned_pair(slab, pair, low * CHUNKS + chunk)

            @pl.loop(1, PEERS)
            def _(step):
                _, owner_there, low, device = across(step)
                pltpu.make_async_remote_copy(
                    src_ref=signal_turned.at[chunk, low * OWNERS + owner_there],
                    dst_ref=signal_in.at[chunk, me],
                    send_sem=signal_send,
                    recv_sem=signal_recv.at[chunk],
                    device_id=device,
                    device_id_type=MESH,
                ).start()

            pltpu.make_async_copy(
                signal_turned.at[chunk, z_lo * OWNERS + owner],
                signal_in.at[chunk, me],
                signal_recv.at[chunk],
            ).start()

    turn = stacked.at[896:1024]

    def transform(source, table, first):
        parts = [
            source[pl.ds(first + u, SIDE, stride=OCTET), :].astype(jnp.bfloat16) for u in range(GROUP)
        ]
        parts = jnp.concatenate(parts, axis=1)
        part = dot(table[...], jnp.concatenate([parts, parts], axis=0))
        cos, sin = turn[:, :SIDE], turn[:, SIDE:]
        turned = []
        for u in range(GROUP):
            real = part[:SIDE, u * SIDE : (u + 1) * SIDE]
            imag = part[SIDE:, u * SIDE : (u + 1) * SIDE]
            turned.append(
                jnp.concatenate([real * cos + imag * sin, imag * cos - real * sin], axis=1)
            )
        turned = jnp.concatenate(turned, axis=0).astype(jnp.bfloat16)
        return dot(turned, into[0]) + dot(turned, into[1])

    def widen(source, target):
        target[...] = source[...].astype(jnp.float32).reshape(target.shape)

    with jax.named_scope("await_filter"):
        pltpu.make_async_copy(filter_mid, filter_mid, filter_recv).wait()
        swap = pltpu.make_async_remote_copy(
            src_ref=filter_mid.at[pl.ds((1 - core) * CHUNKS, CHUNKS)],
            dst_ref=filter_in.at[:, :, core],
            send_sem=swap_send,
            recv_sem=swap_recv.at[0],
            device_id=(owner * CORE + 1 - core, ch),
            device_id_type=MESH,
        )
        swap.start()
        keep = pltpu.make_async_copy(
            filter_mid.at[pl.ds(core * CHUNKS, CHUNKS)], filter_in.at[:, :, core], swap_recv.at[1]
        )
        keep.start()
        keep.wait()
        swap.wait()

    with jax.named_scope("transform_filter"):
        for chunk in range(CHUNKS):
            widen(filter_in.at[chunk], filter_wide)

            @pl.loop(0, OCTET // GROUP)
            def _(group):
                spectrum[chunk, group] = transform(filter_wide, filter_coarse, group * GROUP)

    line = lax.broadcasted_iota(jnp.int32, (OCTET, SIDE), 0)

    for chunk in range(CHUNKS):
        with jax.named_scope(f"await_signal{chunk}"):
            pltpu.make_async_copy(
                signal_in.at[chunk], signal_in.at[chunk], signal_recv.at[chunk]
            ).wait()

        with jax.named_scope(f"convolve{chunk}"):
            widen(signal_in.at[chunk], signal_wide)

            @pl.loop(0, OCTET // GROUP)
            def _(group):
                first = group * GROUP
                wave = transform(signal_wide, signal_coarse, first)
                held = spectrum[chunk, group]
                wave_real, wave_imag = wave[:, :SIDE], wave[:, SIDE:]
                held_real, held_imag = held[:, :SIDE], held[:, SIDE:]
                product = jnp.concatenate(
                    [
                        wave_real * held_real - wave_imag * held_imag,
                        wave_real * held_imag + wave_imag * held_real,
                    ],
                    axis=1,
                ).astype(jnp.bfloat16)
                part = dot(product, outof[0]) + dot(product, outof[1])
                cos, sin = turn[:, :SIDE], turn[:, SIDE:]
                turned = []
                for u in range(GROUP):
                    real = part[u * SIDE : (u + 1) * SIDE, :SIDE]
                    imag = part[u * SIDE : (u + 1) * SIDE, SIDE:]
                    turned.append(
                        jnp.concatenate([real * cos - imag * sin, imag * cos + real * sin], axis=0)
                    )
                turned = jnp.concatenate(turned, axis=1).astype(jnp.bfloat16)
                result = dot(back[0], turned) + dot(back[1], turned)
                for u in range(GROUP):
                    wide[pl.ds(first + u, SIDE, stride=OCTET), :] = result[:, u * SIDE : (u + 1) * SIDE]

            gain = jnp.zeros((OCTET, SIDE), jnp.float32)
            for u in range(OCTET):
                place = (core * CHUNKS + chunk) * SIDE + owner * OCTET + u
                gain = jnp.where(line == u, gain_ref[place], gain)
            mixed = wide[...].reshape(SIDE, OCTET, SIDE) + gain[None] * signal_wide[...].reshape(
                SIDE, OCTET, SIDE
            )
            sent[chunk] = mixed.astype(jnp.bfloat16).reshape(sent.shape[1:])

        with jax.named_scope(f"send_back{chunk}"):

            @pl.loop(1, PEERS)
            def _(step):
                other, _, _, device = across(step)
                pltpu.make_async_remote_copy(
                    src_ref=sent.at[chunk, other],
                    dst_ref=returned.at[chunk, z_lo * OWNERS + owner],
                    send_sem=back_send,
                    recv_sem=back_recv.at[chunk],
                    device_id=device,
                    device_id_type=MESH,
                ).start()

            pltpu.make_async_copy(
                sent.at[chunk, me], returned.at[chunk, z_lo * OWNERS + owner], back_recv.at[chunk]
            ).start()

    for chunk in range(CHUNKS):
        with jax.named_scope(f"await_back{chunk}"):
            pltpu.make_async_copy(returned.at[chunk], returned.at[chunk], back_recv.at[chunk]).wait()

        with jax.named_scope(f"send_out{chunk}"):
            for low in range(Z_LO):
                block = returned[chunk, low * OWNERS : (low + 1) * OWNERS].astype(jnp.float32)
                for tile in range(4):
                    part = block[:, tile * OCTET : (tile + 1) * OCTET, :].reshape(SIDE, SIDE)
                    rows[
                        chunk, tile * SIDE : (tile + 1) * SIDE, low * SIDE : (low + 1) * SIDE
                    ] = part.T.astype(jnp.bfloat16)

            @pl.loop(1, Y * CORE)
            def _(step):
                other_y, other_core, device = aside(step)
                for low in range(Z_LO):
                    pltpu.make_async_remote_copy(
                        src_ref=rows.at[chunk, line_of(other_y, other_core), pl.ds(low * SIDE, SIDE)],
                        dst_ref=out_ref.at[:, columns(low, y, core, chunk * SIDE, SIDE)],
                        send_sem=out_send,
                        recv_sem=out_recv,
                        device_id=device,
                        device_id_type=MESH,
                    ).start()

            for low in range(Z_LO):
                pltpu.make_async_copy(
                    rows.at[chunk, line_of(y, core), pl.ds(low * SIDE, SIDE)],
                    out_ref.at[:, columns(low, y, core, chunk * SIDE, SIDE)],
                    out_recv,
                ).start()

    with jax.named_scope("await_out"):
        pltpu.make_async_copy(out_ref, out_ref, out_recv).wait()

    def settle(part, semaphore):
        pltpu.make_async_copy(part, part, semaphore).wait()

    with jax.named_scope("settle"):
        others = (Y * CORE - 1) * count
        settle(slab.at[pl.ds(0, others)], row_send)
        settle(filter_turned.at[pl.ds(0, OWNERS - 1)], filter_send)
        for chunk in range(CHUNKS):
            settle(signal_turned.at[chunk, pl.ds(0, PEERS - 1)], signal_send)
            settle(sent.at[chunk, pl.ds(0, PEERS - 1)], back_send)
        settle(slab.at[pl.ds(0, others)], out_send)


def shards(query_input, key_input, value_input, filters, direct_gain):
    count, channels = key_input.shape
    table = jnp.asarray(tables())
    stays = pl.BlockSpec(memory_space=pltpu.HBM)
    half, single = jnp.bfloat16, jnp.float32
    span = Y * CORE * count
    octets = (SIDE * OCTET, SIDE)
    dma = pltpu.SemaphoreType.DMA
    mixed = pl.pallas_call(
        kernel,
        out_shape=jax.ShapeDtypeStruct((count, channels), half),
        in_specs=[stays] * 3 + [pl.BlockSpec(memory_space=pltpu.SMEM), stays],
        out_specs=pl.BlockSpec(memory_space=pltpu.VMEM),
        scratch_shapes=[
            pltpu.VMEM((count, channels), half),
            pltpu.VMEM((count, channels), half),
            pltpu.VMEM(filters.shape, half),
            pltpu.VMEM(table.shape, single),
            pltpu.VMEM((2 * SIDE, 2 * SIDE), half),
            pltpu.VMEM((2 * SIDE, 2 * SIDE), half),
            pltpu.VMEM((2, 2 * SIDE, 2 * SIDE), half),
            pltpu.VMEM((2, 2 * SIDE, 2 * SIDE), half),
            pltpu.VMEM((2, SIDE, 2 * SIDE), half),
            pltpu.VMEM((count, channels), half),
            pltpu.VMEM((span, span), half),
            pltpu.VMEM((CHUNKS, PEERS, 4 * OCTET, SIDE), half),
            pltpu.VMEM((CHUNKS, PEERS, 4 * OCTET, SIDE), half),
            pltpu.VMEM((OWNERS, CORE * CHUNKS, 4 * OCTET, SIDE), half),
            pltpu.VMEM((CORE * CHUNKS, OWNERS, 4 * OCTET, SIDE), half),
            pltpu.VMEM((CHUNKS, OWNERS, CORE, 4 * OCTET, SIDE), half),
            pltpu.VMEM(octets, single),
            pltpu.VMEM(octets, single),
            pltpu.VMEM((CHUNKS, OCTET // GROUP, GROUP * SIDE, 2 * SIDE), single),
            pltpu.VMEM(octets, single),
            pltpu.VMEM((CHUNKS, PEERS, 4 * OCTET, SIDE), half),
            pltpu.VMEM((CHUNKS, PEERS, 4 * OCTET, SIDE), half),
            pltpu.VMEM((CHUNKS, span, Z_LO * SIDE), half),
            dma((4,)),
            dma(()),
            dma(()),
            dma(()),
            dma(()),
            dma(()),
            dma((2,)),
            dma(()),
            dma((CHUNKS,)),
            dma(()),
            dma((CHUNKS,)),
            dma(()),
            dma(()),
        ],
        compiler_params=pltpu.CompilerParams(
            collective_id=0, has_side_effects=True, vmem_limit_bytes=60 * 1024 * 1024
        ),
    )(key_input, value_input, filters, direct_gain, table)
    return (query_input.astype(jnp.float32) * mixed.astype(jnp.float32)).astype(jnp.bfloat16)


def solution(mesh):
    return jax.shard_map(
        shards,
        mesh=mesh,
        in_specs=(
            P(("ctx", "ch"), None),
            P(("ctx", "ch"), None),
            P(("ctx", "ch"), None),
            P("ctx", "ch"),
            P("ch"),
        ),
        out_specs=P(("ctx", "ch"), None),
        check_vma=False,
    )
```

profile of v0, /device:TPU:1, one launch (start us, length us, event | category | flops | bytes accessed | tf_op | source)
XLA Modules:
  0.0 58.2 jit_solution(17535750448246846284)
XLA Ops:
  0.0 0.0 copy-start
  0.0 56.2 %shard_map.64 = bf16[64,4096]{1,0:T(8,128)(2,1)} custom-call(bf16[64,4096]{1,0:T(8,128)(2,1)} %key_hbm.1, bf16[64,4096]{1,0:T(8,128)(2,1)} %value_hbm.1, bf16[512,512]{1,0:T(8,128)(2,1)} %filter_hbm.1, f32[512]{0:T(512)} %gain_ref.1, f32[1024,256]{1,0:T(8,128)} %constant.2.clone.tables_hbm), custom_call_target="tpu_custom_call" | custom-call | tf_op jit(solution)/shard_map/pallas_call | solution.py:430
  56.2 0.0 copy-done
  56.2 2.0 %multiply_convert_fusion = bf16[64,4096]{1,0:T(8,128)(2,1)} fusion(bf16[64,4096]{1,0:T(8,128)(2,1)} %shard_map.64, bf16[64,4096]{1,0:T(8,128)(2,1)S(1)} %copy-done), kind=kLoop, calls=%fused_computation | loop fusion | flops 1048576 | bytes 1572864 | tf_op jit(solution)/shard_map/convert_element_type | solution.py:477
Async XLA Ops:
  0.0 56.2 %copy-start = (bf16[64,4096]{1,0:T(8,128)(2,1)S(1)}, bf16[64,4096]{1,0:T(8,128)(2,1)}, u32[]{:S(2)}) copy-start(bf16[64,4096]{1,0:T(8,128)(2,1)} %param.6) | copy-start | bytes 1572868
where the time goes:
time: 58.3 us; the launch traced here: 58.2 us
  Pallas kernels  56.2 us (96%)
  other arithmetic  1.96 us (3%)
    pallas_call x1, Pallas kernels, shards(): pl.pallas_call(kernel, out_shape=jax.ShapeDtypeStruct((count, channels),...  56.2 us
    convert_element_type x1, other arithmetic, shards(): (query_input.astype(jnp.float32) * mixed.astype(jnp.float32)).astype(jnp....  1.96 us

commit v1 on v0

--- a/solution.py
+++ b/solution.py
@@ -26,7 +26,7 @@
     coarse = 2 * np.pi * np.outer(offset, side) / SIDE
     turn = 2 * np.pi * np.outer(offset, side) / length
     fine = 2 * np.pi * np.outer(side, side) / SIDE
-    arrival = side.reshape(OWNERS, CORE, Z_LO, 2).transpose(0, 2, 1, 3).reshape(-1)
+    arrival = side.reshape(OWNERS, CORE, Z_LO, 2).transpose(1, 3, 0, 2).reshape(-1)
 
     def forward(angle):
         return np.concatenate([np.cos(angle), -np.sin(angle)], axis=0)
@@ -82,9 +82,11 @@
     filter_wide,
     spectrum,
     wide,
+    mixed,
+    aside_send,
+    aside_in,
     sent,
     returned,
-    rows,
     load_sems,
     row_send,
     row_recv,
@@ -96,8 +98,8 @@
     signal_recv,
     back_send,
     back_recv,
-    out_send,
-    out_recv,
+    mixed_send,
+    mixed_recv,
 ):
     count = gated.shape[0]
     ctx = lax.axis_index("ctx")
@@ -148,20 +150,25 @@
         def _(step):
             pl.semaphore_signal(barrier, inc=1, device_id=aside(step)[-1], device_id_type=MESH)
 
-    def turned_pair(source, pair, column):
-        parts = []
-        for tile in (2 * pair, 2 * pair + 1):
-            block = source[tile * SIDE : (tile + 1) * SIDE, column * SIDE : (column + 1) * SIDE]
-            parts.append(block.astype(jnp.float32).T.reshape(OWNERS, OCTET, SIDE))
-        return jnp.concatenate(parts, axis=1).astype(jnp.bfloat16)
+    line = lax.broadcasted_iota(jnp.int32, (SIDE, SIDE), 0)
+    lane = lax.broadcasted_iota(jnp.int32, (SIDE, SIDE), 1)
+    place = 64 * ((line >> 1) & 1) + 4 * (line >> 3) + 2 * ((line >> 2) & 1) + (line & 1)
+    pick = jnp.where(lane == place, 1.0, 0.0).astype(jnp.bfloat16)
+
+    def turned(source, column):
+        block = lax.dot_general(
+            pick,
+            source[:, column * SIDE : (column + 1) * SIDE],
+            (((1,), (1,)), ((), ())),
+            preferred_element_type=jnp.float32,
+        )
+        tiles = [block[:, t * SIDE : (t + 1) * SIDE].reshape(OWNERS, OCTET, SIDE) for t in range(4)]
+        return jnp.concatenate(tiles, axis=1).astype(jnp.bfloat16)
 
     with jax.named_scope("turn_filter"):
         loads[0].wait()
         for column in range(CORE * CHUNKS):
-            for pair in range(2):
-                filter_turned[:, column, pair * 16 : (pair + 1) * 16, :] = turned_pair(
-                    filter_ref, pair, column
-                )
+            filter_turned[:, column] = turned(filter_ref, column)
 
     with jax.named_scope("gate"):
         loads[1].wait()
@@ -233,10 +240,9 @@
     with jax.named_scope("send_signal"):
         for chunk in range(CHUNKS):
             for low in range(Z_LO):
-                for pair in range(2):
-                    signal_turned[
-                        chunk, low * OWNERS : (low + 1) * OWNERS, pair * 16 : (pair + 1) * 16, :
-                    ] = turned_pair(slab, pair, low * CHUNKS + chunk)
+                signal_turned[chunk, low * OWNERS : (low + 1) * OWNERS] = turned(
+                    slab, low * CHUNKS + chunk
+                )
 
             @pl.loop(1, PEERS)
             def _(step):
@@ -258,11 +264,8 @@
 
     turn = stacked.at[896:1024]
 
-    def transform(source, table, first):
-        parts = [
-            source[pl.ds(first + u, SIDE, stride=OCTET), :].astype(jnp.bfloat16) for u in range(GROUP)
-        ]
-        parts = jnp.concatenate(parts, axis=1)
+    def transform(parts, table):
+        parts = jnp.concatenate(parts, axis=1).astype(jnp.bfloat16)
         part = dot(table[...], jnp.concatenate([parts, parts], axis=0))
         cos, sin = turn[:, :SIDE], turn[:, SIDE:]
         turned = []
@@ -300,11 +303,62 @@
         for chunk in range(CHUNKS):
             widen(filter_in.at[chunk], filter_wide)
 
-            @pl.loop(0, OCTET // GROUP)
-            def _(group):
-                spectrum[chunk, group] = transform(filter_wide, filter_coarse, group * GROUP)
-
-    line = lax.broadcasted_iota(jnp.int32, (OCTET, SIDE), 0)
+            for group in range(OCTET // GROUP):
+                parts = [
+                    filter_wide[pl.ds(group * GROUP + u, SIDE, stride=OCTET), :] for u in range(GROUP)
+                ]
+                spectrum[chunk, group] = transform(parts, filter_coarse)
+
+    left = lax.broadcasted_iota(jnp.int32, (PEERS, SIDE), 1) < SIDE // 2
+    left_half = lax.broadcasted_iota(jnp.int32, (SIDE // 2, SIDE), 1) < SIDE // 2
+
+    def convolve(chunk, group):
+        parts = [
+            jnp.concatenate(
+                [
+                    signal_wide[pl.ds(tile * OCTET + group * GROUP + u, PEERS, stride=4 * OCTET), :]
+                    for tile in range(4)
+                ],
+                axis=0,
+            )
+            for u in range(GROUP)
+        ]
+        wave = transform(parts, signal_coarse)
+        held = spectrum[chunk, group]
+        wave_real, wave_imag = wave[:, :SIDE], wave[:, SIDE:]
+        held_real, held_imag = held[:, :SIDE], held[:, SIDE:]
+        product = jnp.concatenate(
+            [
+                wave_real * held_real - wave_imag * held_imag,
+                wave_real * held_imag + wave_imag * held_real,
+            ],
+            axis=1,
+        ).astype(jnp.bfloat16)
+        part = dot(product, outof[0]) + dot(product, outof[1])
+        cos, sin = turn[:, :SIDE], turn[:, SIDE:]
+        spun = []
+        for u in range(GROUP):
+            real = part[u * SIDE : (u + 1) * SIDE, :SIDE]
+            imag = part[u * SIDE : (u + 1) * SIDE, SIDE:]
+            spun.append(jnp.concatenate([real * cos - imag * sin, imag * cos + real * sin], axis=0))
+        spun = jnp.concatenate(spun, axis=1).astype(jnp.bfloat16)
+        result = dot(back[0], spun) + dot(back[1], spun)
+        block = (core * CHUNKS + chunk) * SIDE + owner * 4 + group * 2
+        for w in range(2):
+            pair = []
+            for v in range(2):
+                u = 2 * v + w
+                gain = gain_ref[block + 64 * v + w]
+                pair.append(result[:, u * SIDE : (u + 1) * SIDE] + gain * parts[u])
+            for tile in range(4):
+                first, second = (p[tile * PEERS : (tile + 1) * PEERS] for p in pair)
+                mixed[2 * tile, pl.ds(w, PEERS, stride=2), :] = jnp.where(
+                    left, first, pltpu.roll(second, SIDE // 2, 1)
+                )
+                mixed[2 * tile + 1, pl.ds(w, PEERS, stride=2), :] = jnp.where(
+                    left, pltpu.roll(first, SIDE // 2, 1), second
+                )
+        aside_send[chunk, group] = mixed[...].astype(jnp.bfloat16)
 
     for chunk in range(CHUNKS):
         with jax.named_scope(f"await_signal{chunk}"):
@@ -314,45 +368,37 @@
 
         with jax.named_scope(f"convolve{chunk}"):
             widen(signal_in.at[chunk], signal_wide)
-
-            @pl.loop(0, OCTET // GROUP)
-            def _(group):
-                first = group * GROUP
-                wave = transform(signal_wide, signal_coarse, first)
-                held = spectrum[chunk, group]
-                wave_real, wave_imag = wave[:, :SIDE], wave[:, SIDE:]
-                held_real, held_imag = held[:, :SIDE], held[:, SIDE:]
-                product = jnp.concatenate(
-                    [
-                        wave_real * held_real - wave_imag * held_imag,
-                        wave_real * held_imag + wave_imag * held_real,
-                    ],
-                    axis=1,
-                ).astype(jnp.bfloat16)
-                part = dot(product, outof[0]) + dot(product, outof[1])
-                cos, sin = turn[:, :SIDE], turn[:, SIDE:]
-                turned = []
-                for u in range(GROUP):
-                    real = part[u * SIDE : (u + 1) * SIDE, :SIDE]
-                    imag = part[u * SIDE : (u + 1) * SIDE, SIDE:]
-                    turned.append(
-                        jnp.concatenate([real * cos - imag * sin, imag * cos + real * sin], axis=0)
-                    )
-                turned = jnp.concatenate(turned, axis=1).astype(jnp.bfloat16)
-                result = dot(back[0], turned) + dot(back[1], turned)
-                for u in range(GROUP):
-                    wide[pl.ds(first + u, SIDE, stride=OCTET), :] = result[:, u * SIDE : (u + 1) * SIDE]
-
-            gain = jnp.zeros((OCTET, SIDE), jnp.float32)
-            for u in range(OCTET):
-                place = (core * CHUNKS + chunk) * SIDE + owner * OCTET + u
-                gain = jnp.where(line == u, gain_ref[place], gain)
-            mixed = wide[...].reshape(SIDE, OCTET, SIDE) + gain[None] * signal_wide[...].reshape(
-                SIDE, OCTET, SIDE
-            )
-            sent[chunk] = mixed.astype(jnp.bfloat16).reshape(sent.shape[1:])
+            for group in range(OCTET // GROUP):
+                convolve(chunk, group)
+
+                @pl.loop(1, Y * CORE)
+                def _(step):
+                    other_y, other_core, device = aside(step)
+                    pltpu.make_async_remote_copy(
+                        src_ref=aside_send.at[chunk, group, other_core * Y + other_y],
+                        dst_ref=aside_in.at[chunk, group, y * CORE + core],
+                        send_sem=mixed_send,
+                        recv_sem=mixed_recv.at[chunk],
+                        device_id=device,
+                        device_id_type=MESH,
+                    ).start()
+
+                pltpu.make_async_copy(
+                    aside_send.at[chunk, group, core * Y + y],
+                    aside_in.at[chunk, group, y * CORE + core],
+                    mixed_recv.at[chunk],
+                ).start()
 
         with jax.named_scope(f"send_back{chunk}"):
+            pltpu.make_async_copy(aside_in.at[chunk], aside_in.at[chunk], mixed_recv.at[chunk]).wait()
+            widen(aside_in.at[chunk], wide)
+            for peer in range(PEERS):
+                lines = [
+                    wide[pl.ds(group * 512 + peer * 2 + w, OCTET, stride=64), :]
+                    for group in range(2)
+                    for w in range(2)
+                ]
+                sent[chunk, peer] = jnp.concatenate(lines, axis=0).astype(jnp.bfloat16)
 
             @pl.loop(1, PEERS)
             def _(step):
@@ -374,37 +420,24 @@
         with jax.named_scope(f"await_back{chunk}"):
             pltpu.make_async_copy(returned.at[chunk], returned.at[chunk], back_recv.at[chunk]).wait()
 
-        with jax.named_scope(f"send_out{chunk}"):
+        with jax.named_scope(f"finish{chunk}"):
+            widen(returned.at[chunk], wide)
             for low in range(Z_LO):
-                block = returned[chunk, low * OWNERS : (low + 1) * OWNERS].astype(jnp.float32)
-                for tile in range(4):
-                    part = block[:, tile * OCTET : (tile + 1) * OCTET, :].reshape(SIDE, SIDE)
-                    rows[
-                        chunk, tile * SIDE : (tile + 1) * SIDE, low * SIDE : (low + 1) * SIDE
-                    ] = part.T.astype(jnp.bfloat16)
-
-            @pl.loop(1, Y * CORE)
-            def _(step):
-                other_y, other_core, device = aside(step)
-                for low in range(Z_LO):
-                    pltpu.make_async_remote_copy(
-                        src_ref=rows.at[chunk, line_of(other_y, other_core), pl.ds(low * SIDE, SIDE)],
-                        dst_ref=out_ref.at[:, columns(low, y, core, chunk * SIDE, SIDE)],
-                        send_sem=out_send,
-                        recv_sem=out_recv,
-                        device_id=device,
-                        device_id_type=MESH,
-                    ).start()
-
-            for low in range(Z_LO):
-                pltpu.make_async_copy(
-                    rows.at[chunk, line_of(y, core), pl.ds(low * SIDE, SIDE)],
-                    out_ref.at[:, columns(low, y, core, chunk * SIDE, SIDE)],
-                    out_recv,
-                ).start()
-
-    with jax.named_scope("await_out"):
-        pltpu.make_async_copy(out_ref, out_ref, out_recv).wait()
+                for other_y in range(Y):
+                    lines = [
+                        wide[pl.ds(low * 512 + other_y * CORE + c, SIDE // 2, stride=OCTET), :]
+                        for c in range(CORE)
+                    ]
+                    block = jnp.concatenate(lines, axis=0).T
+                    upper, lower = block[: SIDE // 2], block[SIDE // 2 :]
+                    for c, whole in enumerate(
+                        (
+                            jnp.where(left_half, upper, pltpu.roll(lower, SIDE // 2, 1)),
+                            jnp.where(left_half, pltpu.roll(upper, SIDE // 2, 1), lower),
+                        )
+                    ):
+                        start = (half(low, other_y, c) * CHUNKS + chunk) * SIDE
+                        out_ref[:, start : start + SIDE] = whole.astype(jnp.bfloat16)
 
     def settle(part, semaphore):
         pltpu.make_async_copy(part, part, semaphore).wait()
@@ -416,7 +449,8 @@
         for chunk in range(CHUNKS):
             settle(signal_turned.at[chunk, pl.ds(0, PEERS - 1)], signal_send)
             settle(sent.at[chunk, pl.ds(0, PEERS - 1)], back_send)
-        settle(slab.at[pl.ds(0, others)], out_send)
+        for part in range(4):
+            settle(aside_in.at[part // 2, part % 2, pl.ds(0, Y * CORE - 1)], mixed_send)
 
 
 def shards(query_input, key_input, value_input, filters, direct_gain):
@@ -453,9 +487,11 @@
             pltpu.VMEM(octets, single),
             pltpu.VMEM((CHUNKS, OCTET // GROUP, GROUP * SIDE, 2 * SIDE), single),
             pltpu.VMEM(octets, single),
+            pltpu.VMEM((Y * CORE, 2 * PEERS, SIDE), single),
+            pltpu.VMEM((CHUNKS, 2, Y * CORE, 2 * PEERS, SIDE), half),
+            pltpu.VMEM((CHUNKS, 2, Y * CORE, 2 * PEERS, SIDE), half),
             pltpu.VMEM((CHUNKS, PEERS, 4 * OCTET, SIDE), half),
             pltpu.VMEM((CHUNKS, PEERS, 4 * OCTET, SIDE), half),
-            pltpu.VMEM((CHUNKS, span, Z_LO * SIDE), half),
             dma((4,)),
             dma(()),
             dma(()),
@@ -468,7 +504,7 @@
             dma(()),
             dma((CHUNKS,)),
             dma(()),
-            dma(()),
+            dma((CHUNKS,)),
         ],
         compiler_params=pltpu.CompilerParams(
             collective_id=0, has_side_effects=True, vmem_limit_bytes=60 * 1024 * 1024

time: 58.3 us -> 61.6 us (1.057)
  Pallas kernels: 56.2 us -> 59.4 us
    pallas_call x1, Pallas kernels: 56.2 us -> 59.4 us  [shards(): pl.pallas_call(kernel, out_shape=jax.ShapeDtypeStruct((count, channels),...]
where the time goes in v1:
time: 61.6 us; the launch traced here: 61.4 us
  Pallas kernels  59.4 us (96%)
  other arithmetic  1.96 us (3%)
    pallas_call x1, Pallas kernels, shards(): pl.pallas_call(kernel, out_shape=jax.ShapeDtypeStruct((count, channels),...  59.4 us
    convert_element_type x1, other arithmetic, shards(): (query_input.astype(jnp.float32) * mixed.astype(jnp.float32)).astype(jnp....  1.96 us

profile of v1, /device:TPU:1, one launch (start us, length us, event | category | flops | bytes accessed | tf_op | source)
XLA Modules:
  0.0 61.4 jit_solution(13072519535226936909)
XLA Ops:
  0.0 0.0 copy-start
  0.0 59.4 %shard_map.64 = bf16[64,4096]{1,0:T(8,128)(2,1)} custom-call(bf16[64,4096]{1,0:T(8,128)(2,1)} %key_hbm.1, bf16[64,4096]{1,0:T(8,128)(2,1)} %value_hbm.1, bf16[512,512]{1,0:T(8,128)(2,1)} %filter_hbm.1, f32[512]{0:T(512)} %gain_ref.1, f32[1024,256]{1,0:T(8,128)} %constant.2.clone.tables_hbm), custom_call_target="tpu_custom_call" | custom-call | tf_op jit(solution)/shard_map/pallas_call | solution.py:464
  59.5 0.0 copy-done
  59.5 2.0 %multiply_convert_fusion = bf16[64,4096]{1,0:T(8,128)(2,1)} fusion(bf16[64,4096]{1,0:T(8,128)(2,1)} %shard_map.64, bf16[64,4096]{1,0:T(8,128)(2,1)S(1)} %copy-done), kind=kLoop, calls=%fused_computation | loop fusion | flops 1048576 | bytes 1572864 | tf_op jit(solution)/shard_map/convert_element_type | solution.py:513
Async XLA Ops:
  0.0 59.5 %copy-start = (bf16[64,4096]{1,0:T(8,128)(2,1)S(1)}, bf16[64,4096]{1,0:T(8,128)(2,1)}, u32[]{:S(2)}) copy-start(bf16[64,4096]{1,0:T(8,128)(2,1)} %param.6) | copy-start | bytes 1572868

commit v2 on v1

--- a/solution.py
+++ b/solution.py
@@ -85,8 +85,17 @@
     mixed,
     aside_send,
     aside_in,
+    small,
     sent,
+    first_sent,
+    last_sent,
     returned,
+    first_returned,
+    last_returned,
+    rows,
+    first_rows,
+    landed,
+    first_landed,
     load_sems,
     row_send,
     row_recv,
@@ -100,6 +109,8 @@
     back_recv,
     mixed_send,
     mixed_recv,
+    out_send,
+    out_recv,
 ):
     count = gated.shape[0]
     ctx = lax.axis_index("ctx")
@@ -152,12 +163,16 @@
 
     line = lax.broadcasted_iota(jnp.int32, (SIDE, SIDE), 0)
     lane = lax.broadcasted_iota(jnp.int32, (SIDE, SIDE), 1)
-    place = 64 * ((line >> 1) & 1) + 4 * (line >> 3) + 2 * ((line >> 2) & 1) + (line & 1)
-    pick = jnp.where(lane == place, 1.0, 0.0).astype(jnp.bfloat16)
+    place = jnp.where(
+        ((line >> 2) & 1) == 1,
+        64 + 32 * ((line >> 1) & 1) + 2 * (line >> 3) + (line & 1),
+        4 * (line >> 3) + (line & 3),
+    )
+    picks = [jnp.where(lane == p, 1.0, 0.0).astype(jnp.bfloat16) for p in (line, place)]
 
     def turned(source, column):
         block = lax.dot_general(
-            pick,
+            picks[column % CHUNKS],
             source[:, column * SIDE : (column + 1) * SIDE],
             (((1,), (1,)), ((), ())),
             preferred_element_type=jnp.float32,
@@ -310,7 +325,6 @@
                 spectrum[chunk, group] = transform(parts, filter_coarse)
 
     left = lax.broadcasted_iota(jnp.int32, (PEERS, SIDE), 1) < SIDE // 2
-    left_half = lax.broadcasted_iota(jnp.int32, (SIDE // 2, SIDE), 1) < SIDE // 2
 
     def convolve(chunk, group):
         parts = [
@@ -343,101 +357,157 @@
             spun.append(jnp.concatenate([real * cos - imag * sin, imag * cos + real * sin], axis=0))
         spun = jnp.concatenate(spun, axis=1).astype(jnp.bfloat16)
         result = dot(back[0], spun) + dot(back[1], spun)
-        block = (core * CHUNKS + chunk) * SIDE + owner * 4 + group * 2
+        block = (core * CHUNKS + chunk) * SIDE
+        if chunk == 0:
+            places = [block + owner * OCTET + group * GROUP + u for u in range(GROUP)]
+        elif group == 0:
+            places = [block + owner * GROUP + u for u in range(GROUP)]
+        else:
+            places = [block + 64 + 32 * (u // 2) + 2 * owner + u % 2 for u in range(GROUP)]
+        return [
+            result[:, u * SIDE : (u + 1) * SIDE] + gain_ref[places[u]] * parts[u]
+            for u in range(GROUP)
+        ]
+
+    def spread(sums):
         for w in range(2):
-            pair = []
-            for v in range(2):
-                u = 2 * v + w
-                gain = gain_ref[block + 64 * v + w]
-                pair.append(result[:, u * SIDE : (u + 1) * SIDE] + gain * parts[u])
             for tile in range(4):
-                first, second = (p[tile * PEERS : (tile + 1) * PEERS] for p in pair)
+                first, second = (p[tile * PEERS : (tile + 1) * PEERS] for p in (sums[w], sums[2 + w]))
                 mixed[2 * tile, pl.ds(w, PEERS, stride=2), :] = jnp.where(
                     left, first, pltpu.roll(second, SIDE // 2, 1)
                 )
                 mixed[2 * tile + 1, pl.ds(w, PEERS, stride=2), :] = jnp.where(
                     left, pltpu.roll(first, SIDE // 2, 1), second
                 )
-        aside_send[chunk, group] = mixed[...].astype(jnp.bfloat16)
-
-    for chunk in range(CHUNKS):
-        with jax.named_scope(f"await_signal{chunk}"):
-            pltpu.make_async_copy(
-                signal_in.at[chunk], signal_in.at[chunk], signal_recv.at[chunk]
-            ).wait()
-
-        with jax.named_scope(f"convolve{chunk}"):
-            widen(signal_in.at[chunk], signal_wide)
-            for group in range(OCTET // GROUP):
-                convolve(chunk, group)
-
-                @pl.loop(1, Y * CORE)
-                def _(step):
-                    other_y, other_core, device = aside(step)
-                    pltpu.make_async_remote_copy(
-                        src_ref=aside_send.at[chunk, group, other_core * Y + other_y],
-                        dst_ref=aside_in.at[chunk, group, y * CORE + core],
-                        send_sem=mixed_send,
-                        recv_sem=mixed_recv.at[chunk],
-                        device_id=device,
-                        device_id_type=MESH,
-                    ).start()
-
-                pltpu.make_async_copy(
-                    aside_send.at[chunk, group, core * Y + y],
-                    aside_in.at[chunk, group, y * CORE + core],
-                    mixed_recv.at[chunk],
-                ).start()
-
-        with jax.named_scope(f"send_back{chunk}"):
-            pltpu.make_async_copy(aside_in.at[chunk], aside_in.at[chunk], mixed_recv.at[chunk]).wait()
-            widen(aside_in.at[chunk], wide)
-            for peer in range(PEERS):
+
+    def await_signal(chunk):
+        pltpu.make_async_copy(signal_in.at[chunk], signal_in.at[chunk], signal_recv.at[chunk]).wait()
+        widen(signal_in.at[chunk], signal_wide)
+
+    def send_back(source, target, which):
+        @pl.loop(1, PEERS)
+        def _(step):
+            other, _, _, device = across(step)
+            pltpu.make_async_remote_copy(
+                src_ref=source.at[other],
+                dst_ref=target.at[z_lo * OWNERS + owner],
+                send_sem=back_send,
+                recv_sem=back_recv.at[which],
+                device_id=device,
+                device_id_type=MESH,
+            ).start()
+
+        pltpu.make_async_copy(
+            source.at[me], target.at[z_lo * OWNERS + owner], back_recv.at[which]
+        ).start()
+
+    def send_aside(source, target, send_sem, recv_sem):
+        @pl.loop(1, Y * CORE)
+        def _(step):
+            other_y, other_core, device = aside(step)
+            pltpu.make_async_remote_copy(
+                src_ref=source.at[other_core * Y + other_y],
+                dst_ref=target.at[y * CORE + core],
+                send_sem=send_sem,
+                recv_sem=recv_sem,
+                device_id=device,
+                device_id_type=MESH,
+            ).start()
+
+        pltpu.make_async_copy(source.at[core * Y + y], target.at[y * CORE + core], recv_sem).start()
+
+    def arrived(ref, semaphore):
+        pltpu.make_async_copy(ref, ref, semaphore).wait()
+
+    def gather(sums, target, each, first):
+        for u in range(GROUP):
+            for tile in range(4):
+                target[pl.ds(tile * each + first + u, PEERS, stride=4 * each), :] = sums[u][
+                    tile * PEERS : (tile + 1) * PEERS
+                ]
+
+    with jax.named_scope("convolve0"):
+        await_signal(0)
+        for group in range(OCTET // GROUP):
+            gather(convolve(0, group), wide, OCTET, group * GROUP)
+        sent[...] = wide[...].astype(jnp.bfloat16).reshape(sent.shape)
+        send_back(sent, returned, 0)
+
+    with jax.named_scope("convolve1"):
+        await_signal(1)
+        spread(convolve(1, 1))
+        aside_send[...] = mixed[...].astype(jnp.bfloat16)
+        send_aside(aside_send, aside_in, mixed_send, mixed_recv)
+        gather(convolve(1, 0), small, GROUP, 0)
+        first_sent[...] = small[...].astype(jnp.bfloat16).reshape(first_sent.shape)
+        send_back(first_sent, first_returned, 1)
+
+    with jax.named_scope("relay1"):
+        arrived(aside_in, mixed_recv)
+        widen(aside_in, small)
+        for peer in range(PEERS):
+            lines = [small[pl.ds(peer * 2 + w, OCTET, stride=64), :] for w in range(2)]
+            last_sent[peer] = jnp.concatenate(lines, axis=0).astype(jnp.bfloat16)
+        send_back(last_sent, last_returned, 2)
+
+    with jax.named_scope("send_out0"):
+        arrived(returned, back_recv.at[0])
+        for low in range(Z_LO):
+            block = returned[low * OWNERS : (low + 1) * OWNERS].astype(jnp.float32)
+            for tile in range(4):
+                part = block[:, tile * OCTET : (tile + 1) * OCTET, :].reshape(SIDE, SIDE)
+                rows[2 * tile : 2 * tile + 2, :, low * SIDE : (low + 1) * SIDE] = part.T.astype(
+                    jnp.bfloat16
+                ).reshape(2, count, SIDE)
+        send_aside(rows, landed, out_send, out_recv.at[0])
+
+    with jax.named_scope("send_out1"):
+        arrived(first_returned, back_recv.at[1])
+        widen(first_returned, small)
+        blocks = small[...].reshape(PEERS, 4, GROUP, SIDE)
+        for tile in range(4):
+            part = blocks[:, tile].reshape(SIDE, SIDE)
+            first_rows[2 * tile : 2 * tile + 2] = part.T.astype(jnp.bfloat16).reshape(2, count, SIDE)
+        send_aside(first_rows, first_landed, out_send, out_recv.at[1])
+
+    def put(low, other, chunk, block):
+        start = ((low * Y * CORE + other) * CHUNKS + chunk) * SIDE
+        out_ref[:, start : start + SIDE] = block
+
+    with jax.named_scope("finish0"):
+        arrived(landed, out_recv.at[0])
+        for low in range(Z_LO):
+            for other in range(Y * CORE):
+                put(low, other, 0, landed[other, :, low * SIDE : (low + 1) * SIDE])
+
+    quarter = lax.broadcasted_iota(jnp.int32, (count, SIDE), 1) // 32
+    with jax.named_scope("finish1"):
+        arrived(last_returned, back_recv.at[2])
+        widen(last_returned, small)
+        lasts = {}
+        for low in range(Z_LO):
+            for four in range(2):
                 lines = [
-                    wide[pl.ds(group * 512 + peer * 2 + w, OCTET, stride=64), :]
-                    for group in range(2)
-                    for w in range(2)
+                    small[pl.ds(low * 256 + four * 4 + k, PEERS, stride=OCTET), :] for k in range(4)
                 ]
-                sent[chunk, peer] = jnp.concatenate(lines, axis=0).astype(jnp.bfloat16)
-
-            @pl.loop(1, PEERS)
-            def _(step):
-                other, _, _, device = across(step)
-                pltpu.make_async_remote_copy(
-                    src_ref=sent.at[chunk, other],
-                    dst_ref=returned.at[chunk, z_lo * OWNERS + owner],
-                    send_sem=back_send,
-                    recv_sem=back_recv.at[chunk],
-                    device_id=device,
-                    device_id_type=MESH,
-                ).start()
-
-            pltpu.make_async_copy(
-                sent.at[chunk, me], returned.at[chunk, z_lo * OWNERS + owner], back_recv.at[chunk]
-            ).start()
-
-    for chunk in range(CHUNKS):
-        with jax.named_scope(f"await_back{chunk}"):
-            pltpu.make_async_copy(returned.at[chunk], returned.at[chunk], back_recv.at[chunk]).wait()
-
-        with jax.named_scope(f"finish{chunk}"):
-            widen(returned.at[chunk], wide)
+                block = jnp.concatenate(lines, axis=0).T
+                upper, lower = block[:count], block[count:]
+                for k in range(4):
+                    lasts[low, four * 4 + k] = jnp.where(
+                        quarter == 2,
+                        upper if k == 2 else pltpu.roll(upper, (64 - 32 * k) % SIDE, 1),
+                        lower if k == 3 else pltpu.roll(lower, (96 - 32 * k) % SIDE, 1),
+                    )
+        arrived(first_landed, out_recv.at[1])
+        for other in range(Y * CORE):
+            first = first_landed[other].astype(jnp.float32)
             for low in range(Z_LO):
-                for other_y in range(Y):
-                    lines = [
-                        wide[pl.ds(low * 512 + other_y * CORE + c, SIDE // 2, stride=OCTET), :]
-                        for c in range(CORE)
-                    ]
-                    block = jnp.concatenate(lines, axis=0).T
-                    upper, lower = block[: SIDE // 2], block[SIDE // 2 :]
-                    for c, whole in enumerate(
-                        (
-                            jnp.where(left_half, upper, pltpu.roll(lower, SIDE // 2, 1)),
-                            jnp.where(left_half, pltpu.roll(upper, SIDE // 2, 1), lower),
-                        )
-                    ):
-                        start = (half(low, other_y, c) * CHUNKS + chunk) * SIDE
-                        out_ref[:, start : start + SIDE] = whole.astype(jnp.bfloat16)
+                whole = jnp.where(
+                    quarter < 2,
+                    pltpu.roll(first, SIDE // 2, 1) if low else first,
+                    lasts[low, other],
+                )
+                put(low, other, 1, whole.astype(jnp.bfloat16))
 
     def settle(part, semaphore):
         pltpu.make_async_copy(part, part, semaphore).wait()
@@ -448,9 +518,11 @@
         settle(filter_turned.at[pl.ds(0, OWNERS - 1)], filter_send)
         for chunk in range(CHUNKS):
             settle(signal_turned.at[chunk, pl.ds(0, PEERS - 1)], signal_send)
-            settle(sent.at[chunk, pl.ds(0, PEERS - 1)], back_send)
-        for part in range(4):
-            settle(aside_in.at[part // 2, part % 2, pl.ds(0, Y * CORE - 1)], mixed_send)
+        for source in (sent, first_sent, last_sent):
+            settle(source.at[pl.ds(0, PEERS - 1)], back_send)
+        settle(aside_send.at[pl.ds(0, Y * CORE - 1)], mixed_send)
+        for source in (rows, first_rows):
+            settle(source.at[pl.ds(0, Y * CORE - 1)], out_send)
 
 
 def shards(query_input, key_input, value_input, filters, direct_gain):
@@ -488,10 +560,19 @@
             pltpu.VMEM((CHUNKS, OCTET // GROUP, GROUP * SIDE, 2 * SIDE), single),
             pltpu.VMEM(octets, single),
             pltpu.VMEM((Y * CORE, 2 * PEERS, SIDE), single),
-            pltpu.VMEM((CHUNKS, 2, Y * CORE, 2 * PEERS, SIDE), half),
-            pltpu.VMEM((CHUNKS, 2, Y * CORE, 2 * PEERS, SIDE), half),
-            pltpu.VMEM((CHUNKS, PEERS, 4 * OCTET, SIDE), half),
-            pltpu.VMEM((CHUNKS, PEERS, 4 * OCTET, SIDE), half),
+            pltpu.VMEM((Y * CORE, 2 * PEERS, SIDE), half),
+            pltpu.VMEM((Y * CORE, 2 * PEERS, SIDE), half),
+            pltpu.VMEM((SIDE * GROUP, SIDE), single),
+            pltpu.VMEM((PEERS, 4 * OCTET, SIDE), half),
+            pltpu.VMEM((PEERS, 4 * GROUP, SIDE), half),
+            pltpu.VMEM((PEERS, 4 * GROUP, SIDE), half),
+            pltpu.VMEM((PEERS, 4 * OCTET, SIDE), half),
+            pltpu.VMEM((PEERS, 4 * GROUP, SIDE), half),
+            pltpu.VMEM((PEERS, 4 * GROUP, SIDE), half),
+            pltpu.VMEM((Y * CORE, count, Z_LO * SIDE), half),
+            pltpu.VMEM((Y * CORE, count, SIDE), half),
+            pltpu.VMEM((Y * CORE, count, Z_LO * SIDE), half),
+            pltpu.VMEM((Y * CORE, count, SIDE), half),
             dma((4,)),
             dma(()),
             dma(()),
@@ -502,12 +583,14 @@
             dma(()),
             dma((CHUNKS,)),
             dma(()),
-            dma((CHUNKS,)),
-            dma(()),
-            dma((CHUNKS,)),
+            dma((3,)),
+            dma(()),
+            dma(()),
+            dma(()),
+            dma((2,)),
         ],
         compiler_params=pltpu.CompilerParams(
-            collective_id=0, has_side_effects=True, vmem_limit_bytes=60 * 1024 * 1024
+            collective_id=0, has_side_effects=True, vmem_limit_bytes=56000000
         ),
     )(key_input, value_input, filters, direct_gain, table)
     return (query_input.astype(jnp.float32) * mixed.astype(jnp.float32)).astype(jnp.bfloat16)

time: 61.6 us -> 54.8 us (0.89)
  Pallas kernels: 59.4 us -> 53 us
  other arithmetic: 1.96 us -> 0.92 us
  local copies, waits for them, and re-layouts: 0.01 us -> 0.68 us
    pallas_call x1, Pallas kernels: 59.4 us -> 53 us  [shards(): pl.pallas_call(kernel, out_shape=jax.ShapeDtypeStruct((count, channels),...]
    convert_element_type x1, other arithmetic: 1.96 us -> 0.92 us  [shards(): (query_input.astype(jnp.float32) * mixed.astype(jnp.float32)).astype(jnp....]
    unnamed x2 -> x4, local copies, waits for them, and re-layouts: 0.01 us -> 0.68 us
where the time goes in v2:
time: 54.8 us; the launch traced here: 54.7 us
  Pallas kernels  53 us (97%)
  other arithmetic  0.92 us (2%)
  local copies, waits for them, and re-layouts  0.68 us (1%)
    pallas_call x1, Pallas kernels, shards(): pl.pallas_call(kernel, out_shape=jax.ShapeDtypeStruct((count, channels),...  53 us

profile of v2, /device:TPU:1, one launch (start us, length us, event | category | flops | bytes accessed | tf_op | source)
XLA Modules:
  0.0 54.7 jit_solution(4097129335930967845)
XLA Ops:
  0.0 0.0 copy-start
  0.0 0.7 %copy-done = f32[512]{0:T(512)S(1)} copy-done((f32[512]{0:T(512)S(1)}, f32[512]{0:T(512)}, u32[]{:S(2)}) %copy-start) | copy-done | bytes 2072
  0.7 0.0 copy-start.1
  0.7 53.0 %shard_map.64 = bf16[64,4096]{1,0:T(8,128)(2,1)S(1)} custom-call(bf16[64,4096]{1,0:T(8,128)(2,1)} %key_hbm.1, bf16[64,4096]{1,0:T(8,128)(2,1)} %value_hbm.1, bf16[512,512]{1,0:T(8,128)(2,1)} %filter_hbm.1, f32[512]{0:T(512)S(1)} %copy-done, f32[1024,256]{1,0:T(8,128)} %constant.2.clone.tables_hbm), custom_call_target="tpu_custom_call" | custom-call | tf_op jit(solution)/shard_map/pallas_call | solution.py:536
  53.7 0.0 copy-done.1
  53.7 0.9 %multiply_convert_fusion = bf16[64,4096]{1,0:T(8,128)(2,1)} fusion(bf16[64,4096]{1,0:T(8,128)(2,1)S(1)} %shard_map.64, bf16[64,4096]{1,0:T(8,128)(2,1)S(1)} %copy-done.1), kind=kLoop, calls=%fused_computation | loop fusion | flops 1048576 | bytes 1572864 | tf_op jit(solution)/shard_map/convert_element_type | solution.py:596
Async XLA Ops:
  0.0 0.7 %copy-start = (f32[512]{0:T(512)S(1)}, f32[512]{0:T(512)}, u32[]{:S(2)}) copy-start(f32[512]{0:T(512)} %gain_ref.1) | copy-start | bytes 6148
  0.7 53.1 %copy-start.1 = (bf16[64,4096]{1,0:T(8,128)(2,1)S(1)}, bf16[64,4096]{1,0:T(8,128)(2,1)}, u32[]{:S(2)}) copy-start(bf16[64,4096]{1,0:T(8,128)(2,1)} %param.6) | copy-start | bytes 1572868

commit v3 on v2

--- a/solution.py
+++ b/solution.py
@@ -246,8 +246,9 @@
         for target, start in ((signal_coarse, 0), (filter_coarse, SIDE)):
             high, low = halves(stacked[:256, start : start + SIDE])
             target[:, :SIDE], target[:, SIDE:] = high, low
-        for target, start in ((into, 256), (outof, 512), (back, 768)):
+        for target, start in ((into, 256), (back, 768)):
             target[0], target[1] = halves(stacked[start : start + target.shape[1]])
+        outof[...] = stacked[512:768].astype(jnp.bfloat16)
 
     with jax.named_scope("await_rows"):
         pltpu.make_async_copy(slab, slab, row_recv).wait()
@@ -279,7 +280,7 @@
 
     turn = stacked.at[896:1024]
 
-    def transform(parts, table):
+    def transform(parts, table, passes):
         parts = jnp.concatenate(parts, axis=1).astype(jnp.bfloat16)
         part = dot(table[...], jnp.concatenate([parts, parts], axis=0))
         cos, sin = turn[:, :SIDE], turn[:, SIDE:]
@@ -291,7 +292,7 @@
                 jnp.concatenate([real * cos + imag * sin, imag * cos - real * sin], axis=1)
             )
         turned = jnp.concatenate(turned, axis=0).astype(jnp.bfloat16)
-        return dot(turned, into[0]) + dot(turned, into[1])
+        return sum(dot(turned, into[k]) for k in range(passes))
 
     def widen(source, target):
         target[...] = source[...].astype(jnp.float32).reshape(target.shape)
@@ -322,7 +323,7 @@
                 parts = [
                     filter_wide[pl.ds(group * GROUP + u, SIDE, stride=OCTET), :] for u in range(GROUP)
                 ]
-                spectrum[chunk, group] = transform(parts, filter_coarse)
+                spectrum[chunk, group] = transform(parts, filter_coarse, 2)
 
     left = lax.broadcasted_iota(jnp.int32, (PEERS, SIDE), 1) < SIDE // 2
 
@@ -337,7 +338,7 @@
             )
             for u in range(GROUP)
         ]
-        wave = transform(parts, signal_coarse)
+        wave = transform(parts, signal_coarse, 1)
         held = spectrum[chunk, group]
         wave_real, wave_imag = wave[:, :SIDE], wave[:, SIDE:]
         held_real, held_imag = held[:, :SIDE], held[:, SIDE:]
@@ -348,7 +349,7 @@
             ],
             axis=1,
         ).astype(jnp.bfloat16)
-        part = dot(product, outof[0]) + dot(product, outof[1])
+        part = dot(product, outof[...])
         cos, sin = turn[:, :SIDE], turn[:, SIDE:]
         spun = []
         for u in range(GROUP):
@@ -546,7 +547,7 @@
             pltpu.VMEM((2 * SIDE, 2 * SIDE), half),
             pltpu.VMEM((2 * SIDE, 2 * SIDE), half),
             pltpu.VMEM((2, 2 * SIDE, 2 * SIDE), half),
-            pltpu.VMEM((2, 2 * SIDE, 2 * SIDE), half),
+            pltpu.VMEM((2 * SIDE, 2 * SIDE), half),
             pltpu.VMEM((2, SIDE, 2 * SIDE), half),
             pltpu.VMEM((count, channels), half),
             pltpu.VMEM((span, span), half),
@@ -592,7 +593,7 @@
         compiler_params=pltpu.CompilerParams(
             collective_id=0, has_side_effects=True, vmem_limit_bytes=56000000
         ),
-    )(key_input, value_input, filters, direct_gain, table)
+    )(key_input, value_input, filters, pltpu.with_memory_space_constraint(direct_gain, pltpu.HBM), table)
     return (query_input.astype(jnp.float32) * mixed.astype(jnp.float32)).astype(jnp.bfloat16)
 
 

time: 54.8 us -> 54.1 us (0.987)
  local copies, waits for them, and re-layouts: 0.68 us -> 0.01 us
    unnamed x4 -> x2, local copies, waits for them, and re-layouts: 0.68 us -> 0.01 us
where the time goes in v3:
time: 54.1 us; the launch traced here: 54 us
  Pallas kernels  53.1 us (98%)
  other arithmetic  0.92 us (2%)
    pallas_call x1, Pallas kernels, shards(): pl.pallas_call(kernel, out_shape=jax.ShapeDtypeStruct((count, channels),...  53.1 us

profile of v3, /device:TPU:1, one launch (start us, length us, event | category | flops | bytes accessed | tf_op | source)
XLA Modules:
  0.0 54.0 jit_solution(18269380250657522786)
XLA Ops:
  0.0 0.0 copy-start
  0.0 53.1 %shard_map.64 = bf16[64,4096]{1,0:T(8,128)(2,1)S(1)} custom-call(bf16[64,4096]{1,0:T(8,128)(2,1)} %key_hbm.1, bf16[64,4096]{1,0:T(8,128)(2,1)} %value_hbm.1, bf16[512,512]{1,0:T(8,128)(2,1)} %filter_hbm.1, f32[512]{0:T(512)} %gain_ref.1, f32[1024,256]{1,0:T(8,128)} %constant.2.clone.tables_hbm), custom_call_target="tpu_custom_call" | custom-call | tf_op jit(solution)/shard_map/pallas_call | solution.py:537
  53.1 0.0 copy-done
  53.1 0.9 %multiply_convert_fusion = bf16[64,4096]{1,0:T(8,128)(2,1)} fusion(bf16[64,4096]{1,0:T(8,128)(2,1)S(1)} %shard_map.64, bf16[64,4096]{1,0:T(8,128)(2,1)S(1)} %copy-done), kind=kLoop, calls=%fused_computation | loop fusion | flops 1048576 | bytes 1572864 | tf_op jit(solution)/shard_map/convert_element_type | solution.py:597
Async XLA Ops:
  0.0 53.1 %copy-start = (bf16[64,4096]{1,0:T(8,128)(2,1)S(1)}, bf16[64,4096]{1,0:T(8,128)(2,1)}, u32[]{:S(2)}) copy-start(bf16[64,4096]{1,0:T(8,128)(2,1)} %param.6) | copy-start | bytes 1572868

commit v4 on v3

--- a/solution.py
+++ b/solution.py
@@ -75,6 +75,8 @@
     slab,
     signal_turned,
     signal_in,
+    part_turned,
+    part_in,
     filter_turned,
     filter_mid,
     filter_in,
@@ -163,12 +165,49 @@
 
     line = lax.broadcasted_iota(jnp.int32, (SIDE, SIDE), 0)
     lane = lax.broadcasted_iota(jnp.int32, (SIDE, SIDE), 1)
+    group_of = (line >> 2) & 1
     place = jnp.where(
-        ((line >> 2) & 1) == 1,
+        group_of == 1,
         64 + 32 * ((line >> 1) & 1) + 2 * (line >> 3) + (line & 1),
         4 * (line >> 3) + (line & 3),
     )
     picks = [jnp.where(lane == p, 1.0, 0.0).astype(jnp.bfloat16) for p in (line, place)]
+
+    pairs = []
+    for group in range(2):
+        channel = line & 3
+        if group:
+            place = 64 + 32 * (channel >> 1) + 2 * (line >> 3) + (channel & 1)
+        else:
+            place = 4 * (line >> 3) + channel
+        pairs.append(
+            jnp.concatenate(
+                [
+                    jnp.where((lane == place) & (group_of == tile), 1.0, 0.0).astype(jnp.bfloat16)
+                    for tile in range(2)
+                ],
+                axis=1,
+            )
+        )
+
+    def turned_group(source, column, group):
+        parts = []
+        for pair in range(2):
+            tiles = [
+                source[
+                    (2 * pair + t) * SIDE : (2 * pair + t + 1) * SIDE,
+                    column * SIDE : (column + 1) * SIDE,
+                ]
+                for t in range(2)
+            ]
+            block = lax.dot_general(
+                pairs[group],
+                jnp.concatenate(tiles, axis=1),
+                (((1,), (1,)), ((), ())),
+                preferred_element_type=jnp.float32,
+            )
+            parts.append(block.reshape(OWNERS, OCTET, SIDE))
+        return jnp.concatenate(parts, axis=1).astype(jnp.bfloat16)
 
     def turned(source, column):
         block = lax.dot_general(
@@ -253,30 +292,35 @@
     with jax.named_scope("await_rows"):
         pltpu.make_async_copy(slab, slab, row_recv).wait()
 
+    def send_signal(source, target, which):
+        @pl.loop(1, PEERS)
+        def _(step):
+            _, owner_there, low, device = across(step)
+            pltpu.make_async_remote_copy(
+                src_ref=source.at[low * OWNERS + owner_there],
+                dst_ref=target.at[me],
+                send_sem=signal_send,
+                recv_sem=signal_recv.at[which],
+                device_id=device,
+                device_id_type=MESH,
+            ).start()
+
+        pltpu.make_async_copy(
+            source.at[z_lo * OWNERS + owner], target.at[me], signal_recv.at[which]
+        ).start()
+
     with jax.named_scope("send_signal"):
-        for chunk in range(CHUNKS):
+        for group in (None, 1, 0):
             for low in range(Z_LO):
-                signal_turned[chunk, low * OWNERS : (low + 1) * OWNERS] = turned(
-                    slab, low * CHUNKS + chunk
-                )
-
-            @pl.loop(1, PEERS)
-            def _(step):
-                _, owner_there, low, device = across(step)
-                pltpu.make_async_remote_copy(
-                    src_ref=signal_turned.at[chunk, low * OWNERS + owner_there],
-                    dst_ref=signal_in.at[chunk, me],
-                    send_sem=signal_send,
-                    recv_sem=signal_recv.at[chunk],
-                    device_id=device,
-                    device_id_type=MESH,
-                ).start()
-
-            pltpu.make_async_copy(
-                signal_turned.at[chunk, z_lo * OWNERS + owner],
-                signal_in.at[chunk, me],
-                signal_recv.at[chunk],
-            ).start()
+                here = slice(low * OWNERS, (low + 1) * OWNERS)
+                if group is None:
+                    signal_turned[here] = turned(slab, low * CHUNKS)
+                else:
+                    part_turned[group, here] = turned_group(slab, low * CHUNKS + 1, group)
+            if group is None:
+                send_signal(signal_turned, signal_in, 2)
+            else:
+                send_signal(part_turned.at[group], part_in.at[group], group)
 
     turn = stacked.at[896:1024]
 
@@ -328,10 +372,14 @@
     left = lax.broadcasted_iota(jnp.int32, (PEERS, SIDE), 1) < SIDE // 2
 
     def convolve(chunk, group):
+        if chunk == 0:
+            source, each, first = signal_wide, OCTET, group * GROUP
+        else:
+            source, each, first = small, GROUP, 0
         parts = [
             jnp.concatenate(
                 [
-                    signal_wide[pl.ds(tile * OCTET + group * GROUP + u, PEERS, stride=4 * OCTET), :]
+                    source[pl.ds(tile * each + first + u, PEERS, stride=4 * each), :]
                     for tile in range(4)
                 ],
                 axis=0,
@@ -381,10 +429,6 @@
                     left, pltpu.roll(first, SIDE // 2, 1), second
                 )
 
-    def await_signal(chunk):
-        pltpu.make_async_copy(signal_in.at[chunk], signal_in.at[chunk], signal_recv.at[chunk]).wait()
-        widen(signal_in.at[chunk], signal_wide)
-
     def send_back(source, target, which):
         @pl.loop(1, PEERS)
         def _(step):
@@ -428,17 +472,23 @@
                 ]
 
     with jax.named_scope("convolve0"):
-        await_signal(0)
+        arrived(signal_in, signal_recv.at[2])
+        widen(signal_in, signal_wide)
         for group in range(OCTET // GROUP):
             gather(convolve(0, group), wide, OCTET, group * GROUP)
         sent[...] = wide[...].astype(jnp.bfloat16).reshape(sent.shape)
         send_back(sent, returned, 0)
 
-    with jax.named_scope("convolve1"):
-        await_signal(1)
+    with jax.named_scope("convolve_last"):
+        arrived(part_in.at[1], signal_recv.at[1])
+        widen(part_in.at[1], small)
         spread(convolve(1, 1))
         aside_send[...] = mixed[...].astype(jnp.bfloat16)
         send_aside(aside_send, aside_in, mixed_send, mixed_recv)
+
+    with jax.named_scope("convolve1"):
+        arrived(part_in.at[0], signal_recv.at[0])
+        widen(part_in.at[0], small)
         gather(convolve(1, 0), small, GROUP, 0)
         first_sent[...] = small[...].astype(jnp.bfloat16).reshape(first_sent.shape)
         send_back(first_sent, first_returned, 1)
@@ -517,8 +567,8 @@
         others = (Y * CORE - 1) * count
         settle(slab.at[pl.ds(0, others)], row_send)
         settle(filter_turned.at[pl.ds(0, OWNERS - 1)], filter_send)
-        for chunk in range(CHUNKS):
-            settle(signal_turned.at[chunk, pl.ds(0, PEERS - 1)], signal_send)
+        for source in (signal_turned, part_turned.at[0], part_turned.at[1]):
+            settle(source.at[pl.ds(0, PEERS - 1)], signal_send)
         for source in (sent, first_sent, last_sent):
             settle(source.at[pl.ds(0, PEERS - 1)], back_send)
         settle(aside_send.at[pl.ds(0, Y * CORE - 1)], mixed_send)
@@ -551,8 +601,10 @@
             pltpu.VMEM((2, SIDE, 2 * SIDE), half),
             pltpu.VMEM((count, channels), half),
             pltpu.VMEM((span, span), half),
-            pltpu.VMEM((CHUNKS, PEERS, 4 * OCTET, SIDE), half),
-            pltpu.VMEM((CHUNKS, PEERS, 4 * OCTET, SIDE), half),
+            pltpu.VMEM((PEERS, 4 * OCTET, SIDE), half),
+            pltpu.VMEM((PEERS, 4 * OCTET, SIDE), half),
+            pltpu.VMEM((2, PEERS, 4 * GROUP, SIDE), half),
+            pltpu.VMEM((2, PEERS, 4 * GROUP, SIDE), half),
             pltpu.VMEM((OWNERS, CORE * CHUNKS, 4 * OCTET, SIDE), half),
             pltpu.VMEM((CORE * CHUNKS, OWNERS, 4 * OCTET, SIDE), half),
             pltpu.VMEM((CHUNKS, OWNERS, CORE, 4 * OCTET, SIDE), half),
@@ -582,7 +634,7 @@
             dma(()),
             dma((2,)),
             dma(()),
-            dma((CHUNKS,)),
+            dma((3,)),
             dma(()),
             dma((3,)),
             dma(()),

time: 54.1 us -> 53.3 us (0.985)
  Pallas kernels: 53.1 us -> 52.3 us
    pallas_call x1, Pallas kernels: 53.1 us -> 52.3 us  [shards(): pl.pallas_call(kernel, out_shape=jax.ShapeDtypeStruct((count, channels),...]
where the time goes in v4:
time: 53.3 us; the launch traced here: 53.2 us
  Pallas kernels  52.3 us (98%)
  other arithmetic  0.92 us (2%)
    pallas_call x1, Pallas kernels, shards(): pl.pallas_call(kernel, out_shape=jax.ShapeDtypeStruct((count, channels),...  52.3 us

profile of v4, /device:TPU:1, one launch (start us, length us, event | category | flops | bytes accessed | tf_op | source)
XLA Modules:
  0.0 53.2 jit_solution(16318323212103479554)
XLA Ops:
  0.0 0.0 copy-start
  0.0 52.3 %shard_map.64 = bf16[64,4096]{1,0:T(8,128)(2,1)S(1)} custom-call(bf16[64,4096]{1,0:T(8,128)(2,1)} %key_hbm.1, bf16[64,4096]{1,0:T(8,128)(2,1)} %value_hbm.1, bf16[512,512]{1,0:T(8,128)(2,1)} %filter_hbm.1, f32[512]{0:T(512)} %gain_ref.1, f32[1024,256]{1,0:T(8,128)} %constant.2.clone.tables_hbm), custom_call_target="tpu_custom_call" | custom-call | tf_op jit(solution)/shard_map/pallas_call | solution.py:587
  52.3 0.0 copy-done
  52.3 0.9 %multiply_convert_fusion = bf16[64,4096]{1,0:T(8,128)(2,1)} fusion(bf16[64,4096]{1,0:T(8,128)(2,1)S(1)} %shard_map.64, bf16[64,4096]{1,0:T(8,128)(2,1)S(1)} %copy-done), kind=kLoop, calls=%fused_computation | loop fusion | flops 1048576 | bytes 1572864 | tf_op jit(solution)/shard_map/convert_element_type | solution.py:649
Async XLA Ops:
  0.0 52.3 %copy-start = (bf16[64,4096]{1,0:T(8,128)(2,1)S(1)}, bf16[64,4096]{1,0:T(8,128)(2,1)}, u32[]{:S(2)}) copy-start(bf16[64,4096]{1,0:T(8,128)(2,1)} %param.6) | copy-start | bytes 1572868

commit v5 on v4

--- a/solution.py
+++ b/solution.py
@@ -17,6 +17,7 @@
 OWNERS = X * Z_HI
 PEERS = OWNERS * Z_LO
 CHUNKS = 2
+ORDER = 0, 1, 3, 2
 
 
 def tables():
@@ -73,31 +74,21 @@
     back,
     gated,
     slab,
-    signal_turned,
-    signal_in,
     part_turned,
     part_in,
     filter_turned,
     filter_mid,
     filter_in,
-    signal_wide,
     filter_wide,
     spectrum,
-    wide,
     mixed,
     aside_send,
     aside_in,
     small,
     sent,
-    first_sent,
-    last_sent,
     returned,
-    first_returned,
-    last_returned,
     rows,
-    first_rows,
     landed,
-    first_landed,
     load_sems,
     row_send,
     row_recv,
@@ -166,20 +157,19 @@
     line = lax.broadcasted_iota(jnp.int32, (SIDE, SIDE), 0)
     lane = lax.broadcasted_iota(jnp.int32, (SIDE, SIDE), 1)
     group_of = (line >> 2) & 1
+    direct = 64 * group_of + 4 * (line >> 3) + (line & 3)
     place = jnp.where(
-        group_of == 1,
-        64 + 32 * ((line >> 1) & 1) + 2 * (line >> 3) + (line & 1),
-        4 * (line >> 3) + (line & 3),
+        group_of == 1, 64 + 32 * ((line >> 1) & 1) + 2 * (line >> 3) + (line & 1), direct
     )
-    picks = [jnp.where(lane == p, 1.0, 0.0).astype(jnp.bfloat16) for p in (line, place)]
+    picks = [jnp.where(lane == p, 1.0, 0.0).astype(jnp.bfloat16) for p in (direct, place)]
 
     pairs = []
-    for group in range(2):
+    for group in range(4):
         channel = line & 3
-        if group:
+        if group == 3:
             place = 64 + 32 * (channel >> 1) + 2 * (line >> 3) + (channel & 1)
         else:
-            place = 4 * (line >> 3) + channel
+            place = 64 * (group % 2) + 4 * (line >> 3) + channel
         pairs.append(
             jnp.concatenate(
                 [
@@ -190,16 +180,10 @@
             )
         )
 
-    def turned_group(source, column, group):
+    def turned_group(source, group):
         parts = []
         for pair in range(2):
-            tiles = [
-                source[
-                    (2 * pair + t) * SIDE : (2 * pair + t + 1) * SIDE,
-                    column * SIDE : (column + 1) * SIDE,
-                ]
-                for t in range(2)
-            ]
+            tiles = [source[(2 * pair + t) * SIDE : (2 * pair + t + 1) * SIDE] for t in range(2)]
             block = lax.dot_general(
                 pairs[group],
                 jnp.concatenate(tiles, axis=1),
@@ -221,8 +205,9 @@
 
     with jax.named_scope("turn_filter"):
         loads[0].wait()
-        for column in range(CORE * CHUNKS):
-            filter_turned[:, column] = turned(filter_ref, column)
+        for there in range(CORE):
+            for chunk in range(CHUNKS):
+                filter_turned[:, chunk, there] = turned(filter_ref, there * CHUNKS + chunk)
 
     with jax.named_scope("gate"):
         loads[1].wait()
@@ -234,21 +219,25 @@
     with jax.named_scope("await_greet"):
         pl.semaphore_wait(barrier, PEERS + Y * CORE - 2)
 
-    with jax.named_scope("send_filter"):
-
+    def send_filter(chunk):
         @pl.loop(1, OWNERS)
         def _(step):
             other, device = owners(step)
             pltpu.make_async_remote_copy(
-                src_ref=filter_turned.at[other],
-                dst_ref=filter_mid.at[:, owner],
+                src_ref=filter_turned.at[other, chunk],
+                dst_ref=filter_mid.at[chunk, :, owner],
                 send_sem=filter_send,
-                recv_sem=filter_recv,
+                recv_sem=filter_recv.at[chunk],
                 device_id=device,
                 device_id_type=MESH,
             ).start()
 
-        pltpu.make_async_copy(filter_turned.at[owner], filter_mid.at[:, owner], filter_recv).start()
+        pltpu.make_async_copy(
+            filter_turned.at[owner, chunk], filter_mid.at[chunk, :, owner], filter_recv.at[chunk]
+        ).start()
+
+    with jax.named_scope("send_filter"):
+        send_filter(0)
 
     def columns(low, other_y, other_core, first, size):
         start = half(low, other_y, other_core) * CHUNKS * SIDE + first
@@ -258,27 +247,30 @@
         return pl.ds(pl.multiple_of((other_core * Y + other_y) * count, count), count)
 
     with jax.named_scope("send_rows"):
-        span = CHUNKS * SIDE
-
-        @pl.loop(1, Y * CORE)
-        def _(step):
-            other_y, other_core, device = aside(step)
+        for chunk in range(CHUNKS):
+
+            @pl.loop(1, Y * CORE)
+            def _(step):
+                other_y, other_core, device = aside(step)
+                for low in range(Z_LO):
+                    pltpu.make_async_remote_copy(
+                        src_ref=gated.at[:, columns(low, other_y, other_core, chunk * SIDE, SIDE)],
+                        dst_ref=slab.at[chunk, low, line_of(y, core), :],
+                        send_sem=row_send,
+                        recv_sem=row_recv.at[chunk],
+                        device_id=device,
+                        device_id_type=MESH,
+                    ).start()
+
             for low in range(Z_LO):
-                pltpu.make_async_remote_copy(
-                    src_ref=gated.at[:, columns(low, other_y, other_core, 0, span)],
-                    dst_ref=slab.at[line_of(y, core), pl.ds(low * span, span)],
-                    send_sem=row_send,
-                    recv_sem=row_recv,
-                    device_id=device,
-                    device_id_type=MESH,
+                pltpu.make_async_copy(
+                    gated.at[:, columns(low, y, core, chunk * SIDE, SIDE)],
+                    slab.at[chunk, low, line_of(y, core), :],
+                    row_recv.at[chunk],
                 ).start()
 
-        for low in range(Z_LO):
-            pltpu.make_async_copy(
-                gated.at[:, columns(low, y, core, 0, span)],
-                slab.at[line_of(y, core), pl.ds(low * span, span)],
-                row_recv,
-            ).start()
+    with jax.named_scope("send_filter1"):
+        send_filter(1)
 
     with jax.named_scope("split_tables"):
         loads[3].wait()
@@ -288,9 +280,6 @@
         for target, start in ((into, 256), (back, 768)):
             target[0], target[1] = halves(stacked[start : start + target.shape[1]])
         outof[...] = stacked[512:768].astype(jnp.bfloat16)
-
-    with jax.named_scope("await_rows"):
-        pltpu.make_async_copy(slab, slab, row_recv).wait()
 
     def send_signal(source, target, which):
         @pl.loop(1, PEERS)
@@ -309,18 +298,17 @@
             source.at[z_lo * OWNERS + owner], target.at[me], signal_recv.at[which]
         ).start()
 
-    with jax.named_scope("send_signal"):
-        for group in (None, 1, 0):
+    def send_signals(chunk, groups):
+        pltpu.make_async_copy(slab.at[chunk], slab.at[chunk], row_recv.at[chunk]).wait()
+        for group in groups:
             for low in range(Z_LO):
                 here = slice(low * OWNERS, (low + 1) * OWNERS)
-                if group is None:
-                    signal_turned[here] = turned(slab, low * CHUNKS)
-                else:
-                    part_turned[group, here] = turned_group(slab, low * CHUNKS + 1, group)
-            if group is None:
-                send_signal(signal_turned, signal_in, 2)
-            else:
-                send_signal(part_turned.at[group], part_in.at[group], group)
+                part_turned[group, here] = turned_group(slab[chunk, low], group)
+            send_signal(part_turned.at[group], part_in.at[group], group)
+
+    with jax.named_scope("send_signal"):
+        send_signals(0, ORDER[:2])
+        send_signals(1, ORDER[2:])
 
     turn = stacked.at[896:1024]
 
@@ -341,45 +329,45 @@
     def widen(source, target):
         target[...] = source[...].astype(jnp.float32).reshape(target.shape)
 
-    with jax.named_scope("await_filter"):
-        pltpu.make_async_copy(filter_mid, filter_mid, filter_recv).wait()
+    def take_filter(chunk):
+        pltpu.make_async_copy(
+            filter_mid.at[chunk], filter_mid.at[chunk], filter_recv.at[chunk]
+        ).wait()
         swap = pltpu.make_async_remote_copy(
-            src_ref=filter_mid.at[pl.ds((1 - core) * CHUNKS, CHUNKS)],
-            dst_ref=filter_in.at[:, :, core],
+            src_ref=filter_mid.at[chunk, 1 - core],
+            dst_ref=filter_in.at[chunk, :, core],
             send_sem=swap_send,
-            recv_sem=swap_recv.at[0],
+            recv_sem=swap_recv.at[0, chunk],
             device_id=(owner * CORE + 1 - core, ch),
             device_id_type=MESH,
         )
         swap.start()
         keep = pltpu.make_async_copy(
-            filter_mid.at[pl.ds(core * CHUNKS, CHUNKS)], filter_in.at[:, :, core], swap_recv.at[1]
+            filter_mid.at[chunk, core], filter_in.at[chunk, :, core], swap_recv.at[1, chunk]
         )
         keep.start()
         keep.wait()
         swap.wait()
 
-    with jax.named_scope("transform_filter"):
-        for chunk in range(CHUNKS):
-            widen(filter_in.at[chunk], filter_wide)
-
-            for group in range(OCTET // GROUP):
-                parts = [
-                    filter_wide[pl.ds(group * GROUP + u, SIDE, stride=OCTET), :] for u in range(GROUP)
-                ]
-                spectrum[chunk, group] = transform(parts, filter_coarse, 2)
+    def transform_filter(chunk):
+        widen(filter_in.at[chunk], filter_wide)
+        for group in range(OCTET // GROUP):
+            parts = [
+                filter_wide[pl.ds(group * GROUP + u, SIDE, stride=OCTET), :] for u in range(GROUP)
+            ]
+            spectrum[chunk, group] = transform(parts, filter_coarse, 2)
+
+    with jax.named_scope("take_filter0"):
+        take_filter(0)
+        transform_filter(0)
 
     left = lax.broadcasted_iota(jnp.int32, (PEERS, SIDE), 1) < SIDE // 2
 
     def convolve(chunk, group):
-        if chunk == 0:
-            source, each, first = signal_wide, OCTET, group * GROUP
-        else:
-            source, each, first = small, GROUP, 0
         parts = [
             jnp.concatenate(
                 [
-                    source[pl.ds(tile * each + first + u, PEERS, stride=4 * each), :]
+                    small[pl.ds(tile * GROUP + u, PEERS, stride=4 * GROUP), :]
                     for tile in range(4)
                 ],
                 axis=0,
@@ -407,10 +395,8 @@
         spun = jnp.concatenate(spun, axis=1).astype(jnp.bfloat16)
         result = dot(back[0], spun) + dot(back[1], spun)
         block = (core * CHUNKS + chunk) * SIDE
-        if chunk == 0:
-            places = [block + owner * OCTET + group * GROUP + u for u in range(GROUP)]
-        elif group == 0:
-            places = [block + owner * GROUP + u for u in range(GROUP)]
+        if chunk == 0 or group == 0:
+            places = [block + 64 * group + owner * GROUP + u for u in range(GROUP)]
         else:
             places = [block + 64 + 32 * (u // 2) + 2 * owner + u % 2 for u in range(GROUP)]
         return [
@@ -464,77 +450,80 @@
     def arrived(ref, semaphore):
         pltpu.make_async_copy(ref, ref, semaphore).wait()
 
-    def gather(sums, target, each, first):
+    def await_signal(group):
+        arrived(part_in.at[group], signal_recv.at[group])
+        widen(part_in.at[group], small)
+
+    def send_direct(which):
+        await_signal(which)
+        sums = convolve(which // 2, which % 2)
         for u in range(GROUP):
             for tile in range(4):
-                target[pl.ds(tile * each + first + u, PEERS, stride=4 * each), :] = sums[u][
+                small[pl.ds(tile * GROUP + u, PEERS, stride=4 * GROUP), :] = sums[u][
                     tile * PEERS : (tile + 1) * PEERS
                 ]
-
-    with jax.named_scope("convolve0"):
-        arrived(signal_in, signal_recv.at[2])
-        widen(signal_in, signal_wide)
-        for group in range(OCTET // GROUP):
-            gather(convolve(0, group), wide, OCTET, group * GROUP)
-        sent[...] = wide[...].astype(jnp.bfloat16).reshape(sent.shape)
-        send_back(sent, returned, 0)
-
-    with jax.named_scope("convolve_last"):
-        arrived(part_in.at[1], signal_recv.at[1])
-        widen(part_in.at[1], small)
+        sent[which] = small[...].astype(jnp.bfloat16).reshape(sent.shape[1:])
+        send_back(sent.at[which], returned.at[which], which)
+
+    def send_first():
+        await_signal(3)
         spread(convolve(1, 1))
         aside_send[...] = mixed[...].astype(jnp.bfloat16)
         send_aside(aside_send, aside_in, mixed_send, mixed_recv)
 
-    with jax.named_scope("convolve1"):
-        arrived(part_in.at[0], signal_recv.at[0])
-        widen(part_in.at[0], small)
-        gather(convolve(1, 0), small, GROUP, 0)
-        first_sent[...] = small[...].astype(jnp.bfloat16).reshape(first_sent.shape)
-        send_back(first_sent, first_returned, 1)
-
-    with jax.named_scope("relay1"):
+    for group in ORDER:
+        if group == ORDER[2]:
+            with jax.named_scope("take_filter1"):
+                take_filter(1)
+                transform_filter(1)
+
+        with jax.named_scope(f"convolve{group}"):
+            if group < 3:
+                send_direct(group)
+            else:
+                send_first()
+
+    with jax.named_scope("relay"):
         arrived(aside_in, mixed_recv)
         widen(aside_in, small)
         for peer in range(PEERS):
             lines = [small[pl.ds(peer * 2 + w, OCTET, stride=64), :] for w in range(2)]
-            last_sent[peer] = jnp.concatenate(lines, axis=0).astype(jnp.bfloat16)
-        send_back(last_sent, last_returned, 2)
-
-    with jax.named_scope("send_out0"):
-        arrived(returned, back_recv.at[0])
-        for low in range(Z_LO):
-            block = returned[low * OWNERS : (low + 1) * OWNERS].astype(jnp.float32)
+            sent[3, peer] = jnp.concatenate(lines, axis=0).astype(jnp.bfloat16)
+        send_back(sent.at[3], returned.at[3], 3)
+
+    for which in range(3):
+        with jax.named_scope(f"send_out{which}"):
+            arrived(returned.at[which], back_recv.at[which])
+            widen(returned.at[which], small)
+            blocks = small[...].reshape(PEERS, 4, GROUP, SIDE)
             for tile in range(4):
-                part = block[:, tile * OCTET : (tile + 1) * OCTET, :].reshape(SIDE, SIDE)
-                rows[2 * tile : 2 * tile + 2, :, low * SIDE : (low + 1) * SIDE] = part.T.astype(
-                    jnp.bfloat16
-                ).reshape(2, count, SIDE)
-        send_aside(rows, landed, out_send, out_recv.at[0])
-
-    with jax.named_scope("send_out1"):
-        arrived(first_returned, back_recv.at[1])
-        widen(first_returned, small)
-        blocks = small[...].reshape(PEERS, 4, GROUP, SIDE)
-        for tile in range(4):
-            part = blocks[:, tile].reshape(SIDE, SIDE)
-            first_rows[2 * tile : 2 * tile + 2] = part.T.astype(jnp.bfloat16).reshape(2, count, SIDE)
-        send_aside(first_rows, first_landed, out_send, out_recv.at[1])
+                part = blocks[:, tile].reshape(SIDE, SIDE)
+                rows[which, 2 * tile : 2 * tile + 2] = part.T.astype(jnp.bfloat16).reshape(
+                    2, count, SIDE
+                )
+            send_aside(rows.at[which], landed.at[which], out_send, out_recv.at[which])
 
     def put(low, other, chunk, block):
         start = ((low * Y * CORE + other) * CHUNKS + chunk) * SIDE
         out_ref[:, start : start + SIDE] = block
 
+    quarter = lax.broadcasted_iota(jnp.int32, (count, SIDE), 1) // 32
     with jax.named_scope("finish0"):
-        arrived(landed, out_recv.at[0])
-        for low in range(Z_LO):
-            for other in range(Y * CORE):
-                put(low, other, 0, landed[other, :, low * SIDE : (low + 1) * SIDE])
-
-    quarter = lax.broadcasted_iota(jnp.int32, (count, SIDE), 1) // 32
+        arrived(landed.at[0], out_recv.at[0])
+        arrived(landed.at[1], out_recv.at[1])
+        for other in range(Y * CORE):
+            first, second = (landed[group, other].astype(jnp.float32) for group in range(2))
+            for low in range(Z_LO):
+                whole = jnp.where(
+                    quarter < 2,
+                    pltpu.roll(first, SIDE // 2, 1) if low else first,
+                    second if low else pltpu.roll(second, SIDE // 2, 1),
+                )
+                put(low, other, 0, whole.astype(jnp.bfloat16))
+
     with jax.named_scope("finish1"):
-        arrived(last_returned, back_recv.at[2])
-        widen(last_returned, small)
+        arrived(returned.at[3], back_recv.at[3])
+        widen(returned.at[3], small)
         lasts = {}
         for low in range(Z_LO):
             for four in range(2):
@@ -549,9 +538,9 @@
                         upper if k == 2 else pltpu.roll(upper, (64 - 32 * k) % SIDE, 1),
                         lower if k == 3 else pltpu.roll(lower, (96 - 32 * k) % SIDE, 1),
                     )
-        arrived(first_landed, out_recv.at[1])
+        arrived(landed.at[2], out_recv.at[2])
         for other in range(Y * CORE):
-            first = first_landed[other].astype(jnp.float32)
+            first = landed[2, other].astype(jnp.float32)
             for low in range(Z_LO):
                 whole = jnp.where(
                     quarter < 2,
@@ -564,16 +553,15 @@
         pltpu.make_async_copy(part, part, semaphore).wait()
 
     with jax.named_scope("settle"):
-        others = (Y * CORE - 1) * count
-        settle(slab.at[pl.ds(0, others)], row_send)
+        for chunk in range(CHUNKS):
+            settle(slab.at[chunk, :, pl.ds(0, (Y * CORE - 1) * count)], row_send)
         settle(filter_turned.at[pl.ds(0, OWNERS - 1)], filter_send)
-        for source in (signal_turned, part_turned.at[0], part_turned.at[1]):
-            settle(source.at[pl.ds(0, PEERS - 1)], signal_send)
-        for source in (sent, first_sent, last_sent):
-            settle(source.at[pl.ds(0, PEERS - 1)], back_send)
+        for which in range(4):
+            settle(part_turned.at[which, pl.ds(0, PEERS - 1)], signal_send)
+            settle(sent.at[which, pl.ds(0, PEERS - 1)], back_send)
         settle(aside_send.at[pl.ds(0, Y * CORE - 1)], mixed_send)
-        for source in (rows, first_rows):
-            settle(source.at[pl.ds(0, Y * CORE - 1)], out_send)
+        for which in range(3):
+            settle(rows.at[which, pl.ds(0, Y * CORE - 1)], out_send)
 
 
 def shards(query_input, key_input, value_input, filters, direct_gain):
@@ -600,47 +588,37 @@
             pltpu.VMEM((2 * SIDE, 2 * SIDE), half),
             pltpu.VMEM((2, SIDE, 2 * SIDE), half),
             pltpu.VMEM((count, channels), half),
-            pltpu.VMEM((span, span), half),
-            pltpu.VMEM((PEERS, 4 * OCTET, SIDE), half),
-            pltpu.VMEM((PEERS, 4 * OCTET, SIDE), half),
-            pltpu.VMEM((2, PEERS, 4 * GROUP, SIDE), half),
-            pltpu.VMEM((2, PEERS, 4 * GROUP, SIDE), half),
-            pltpu.VMEM((OWNERS, CORE * CHUNKS, 4 * OCTET, SIDE), half),
-            pltpu.VMEM((CORE * CHUNKS, OWNERS, 4 * OCTET, SIDE), half),
+            pltpu.VMEM((CHUNKS, Z_LO, span, SIDE), half),
+            pltpu.VMEM((4, PEERS, 4 * GROUP, SIDE), half),
+            pltpu.VMEM((4, PEERS, 4 * GROUP, SIDE), half),
+            pltpu.VMEM((OWNERS, CHUNKS, CORE, 4 * OCTET, SIDE), half),
+            pltpu.VMEM((CHUNKS, CORE, OWNERS, 4 * OCTET, SIDE), half),
             pltpu.VMEM((CHUNKS, OWNERS, CORE, 4 * OCTET, SIDE), half),
             pltpu.VMEM(octets, single),
-            pltpu.VMEM(octets, single),
             pltpu.VMEM((CHUNKS, OCTET // GROUP, GROUP * SIDE, 2 * SIDE), single),
-            pltpu.VMEM(octets, single),
             pltpu.VMEM((Y * CORE, 2 * PEERS, SIDE), single),
             pltpu.VMEM((Y * CORE, 2 * PEERS, SIDE), half),
             pltpu.VMEM((Y * CORE, 2 * PEERS, SIDE), half),
             pltpu.VMEM((SIDE * GROUP, SIDE), single),
-            pltpu.VMEM((PEERS, 4 * OCTET, SIDE), half),
-            pltpu.VMEM((PEERS, 4 * GROUP, SIDE), half),
-            pltpu.VMEM((PEERS, 4 * GROUP, SIDE), half),
-            pltpu.VMEM((PEERS, 4 * OCTET, SIDE), half),
-            pltpu.VMEM((PEERS, 4 * GROUP, SIDE), half),
-            pltpu.VMEM((PEERS, 4 * GROUP, SIDE), half),
-            pltpu.VMEM((Y * CORE, count, Z_LO * SIDE), half),
-            pltpu.VMEM((Y * CORE, count, SIDE), half),
-            pltpu.VMEM((Y * CORE, count, Z_LO * SIDE), half),
-            pltpu.VMEM((Y * CORE, count, SIDE), half),
+            pltpu.VMEM((4, PEERS, 4 * GROUP, SIDE), half),
+            pltpu.VMEM((4, PEERS, 4 * GROUP, SIDE), half),
+            pltpu.VMEM((3, Y * CORE, count, SIDE), half),
+            pltpu.VMEM((3, Y * CORE, count, SIDE), half),
             dma((4,)),
             dma(()),
-            dma(()),
-            dma(()),
-            dma(()),
-            dma(()),
-            dma((2,)),
+            dma((CHUNKS,)),
+            dma(()),
+            dma((CHUNKS,)),
+            dma(()),
+            dma((2, CHUNKS)),
+            dma(()),
+            dma((4,)),
+            dma(()),
+            dma((4,)),
+            dma(()),
+            dma(()),
             dma(()),
             dma((3,)),
-            dma(()),
-            dma((3,)),
-            dma(()),
-            dma(()),
-            dma(()),
-            dma((2,)),
         ],
         compiler_params=pltpu.CompilerParams(
             collective_id=0, has_side_effects=True, vmem_limit_bytes=56000000

time: 53.3 us -> 53 us (level)
  no operation moved by 1% of the time
where the time goes in v5:
time: 53 us; the launch traced here: 52.9 us
  Pallas kernels  52 us (98%)
  other arithmetic  0.92 us (2%)
    pallas_call x1, Pallas kernels, shards(): pl.pallas_call(kernel, out_shape=jax.ShapeDtypeStruct((count, channels),...  52 us

profile of v5, /device:TPU:1, one launch (start us, length us, event | category | flops | bytes accessed | tf_op | source)
XLA Modules:
  0.0 52.9 jit_solution(4670171380268399457)
XLA Ops:
  0.0 0.0 copy-start
  0.0 52.0 %shard_map.64 = bf16[64,4096]{1,0:T(8,128)(2,1)S(1)} custom-call(bf16[64,4096]{1,0:T(8,128)(2,1)} %key_hbm.1, bf16[64,4096]{1,0:T(8,128)(2,1)} %value_hbm.1, bf16[512,512]{1,0:T(8,128)(2,1)} %filter_hbm.1, f32[512]{0:T(512)} %gain_ref.1, f32[1024,256]{1,0:T(8,128)} %constant.2.clone.tables_hbm), custom_call_target="tpu_custom_call" | custom-call | tf_op jit(solution)/shard_map/pallas_call | solution.py:575
  52.0 0.0 copy-done
  52.0 0.9 %multiply_convert_fusion = bf16[64,4096]{1,0:T(8,128)(2,1)} fusion(bf16[64,4096]{1,0:T(8,128)(2,1)S(1)} %shard_map.64, bf16[64,4096]{1,0:T(8,128)(2,1)S(1)} %copy-done), kind=kLoop, calls=%fused_computation | loop fusion | flops 1048576 | bytes 1572864 | tf_op jit(solution)/shard_map/convert_element_type | solution.py:627
Async XLA Ops:
  0.0 52.0 %copy-start = (bf16[64,4096]{1,0:T(8,128)(2,1)S(1)}, bf16[64,4096]{1,0:T(8,128)(2,1)}, u32[]{:S(2)}) copy-start(bf16[64,4096]{1,0:T(8,128)(2,1)} %param.6) | copy-start | bytes 1572868

commit v6 on v5

--- a/solution.py
+++ b/solution.py
@@ -393,7 +393,7 @@
             imag = part[u * SIDE : (u + 1) * SIDE, SIDE:]
             spun.append(jnp.concatenate([real * cos - imag * sin, imag * cos + real * sin], axis=0))
         spun = jnp.concatenate(spun, axis=1).astype(jnp.bfloat16)
-        result = dot(back[0], spun) + dot(back[1], spun)
+        result = dot(back[0], spun)
         block = (core * CHUNKS + chunk) * SIDE
         if chunk == 0 or group == 0:
             places = [block + 64 * group + owner * GROUP + u for u in range(GROUP)]
@@ -491,6 +491,28 @@
             sent[3, peer] = jnp.concatenate(lines, axis=0).astype(jnp.bfloat16)
         send_back(sent.at[3], returned.at[3], 3)
 
+    def send_tile(tile):
+        for upper in range(2):
+            other_core, other_y = tile // 2, 2 * (tile % 2) + upper
+            mine = jnp.logical_and(core == other_core, y == other_y)
+            source = rows.at[2, 2 * tile + upper]
+            target = landed.at[2, y * CORE + core]
+
+            @pl.when(mine)
+            def _():
+                pltpu.make_async_copy(source, target, out_recv.at[2]).start()
+
+            @pl.when(jnp.logical_not(mine))
+            def _():
+                pltpu.make_async_remote_copy(
+                    src_ref=source,
+                    dst_ref=target,
+                    send_sem=out_send,
+                    recv_sem=out_recv.at[2],
+                    device_id=(owner * CORE + other_core, z_lo * Y + other_y),
+                    device_id_type=MESH,
+                ).start()
+
     for which in range(3):
         with jax.named_scope(f"send_out{which}"):
             arrived(returned.at[which], back_recv.at[which])
@@ -501,7 +523,10 @@
                 rows[which, 2 * tile : 2 * tile + 2] = part.T.astype(jnp.bfloat16).reshape(
                     2, count, SIDE
                 )
-            send_aside(rows.at[which], landed.at[which], out_send, out_recv.at[which])
+                if which == 2:
+                    send_tile(tile)
+            if which < 2:
+                send_aside(rows.at[which], landed.at[which], out_send, out_recv.at[which])
 
     def put(low, other, chunk, block):
         start = ((low * Y * CORE + other) * CHUNKS + chunk) * SIDE

time: 53 us -> 52.6 us (level)
  no operation moved by 1% of the time
where the time goes in v6:
time: 52.6 us; the launch traced here: 52.5 us
  Pallas kernels  51.6 us (98%)
  other arithmetic  0.92 us (2%)
    pallas_call x1, Pallas kernels, shards(): pl.pallas_call(kernel, out_shape=jax.ShapeDtypeStruct((count, channels),...  51.6 us

profile of v6, /device:TPU:1, one launch (start us, length us, event | category | flops | bytes accessed | tf_op | source)
XLA Modules:
  0.0 52.5 jit_solution(2803435940075952816)
XLA Ops:
  0.0 0.0 copy-start
  0.0 51.6 %shard_map.64 = bf16[64,4096]{1,0:T(8,128)(2,1)S(1)} custom-call(bf16[64,4096]{1,0:T(8,128)(2,1)} %key_hbm.1, bf16[64,4096]{1,0:T(8,128)(2,1)} %value_hbm.1, bf16[512,512]{1,0:T(8,128)(2,1)} %filter_hbm.1, f32[512]{0:T(512)} %gain_ref.1, f32[1024,256]{1,0:T(8,128)} %constant.2.clone.tables_hbm), custom_call_target="tpu_custom_call" | custom-call | tf_op jit(solution)/shard_map/pallas_call | solution.py:600
  51.6 0.0 copy-done
  51.6 0.9 %multiply_convert_fusion = bf16[64,4096]{1,0:T(8,128)(2,1)} fusion(bf16[64,4096]{1,0:T(8,128)(2,1)S(1)} %shard_map.64, bf16[64,4096]{1,0:T(8,128)(2,1)S(1)} %copy-done), kind=kLoop, calls=%fused_computation | loop fusion | flops 1048576 | bytes 1572864 | tf_op jit(solution)/shard_map/convert_element_type | solution.py:652
Async XLA Ops:
  0.0 51.6 %copy-start = (bf16[64,4096]{1,0:T(8,128)(2,1)S(1)}, bf16[64,4096]{1,0:T(8,128)(2,1)}, u32[]{:S(2)}) copy-start(bf16[64,4096]{1,0:T(8,128)(2,1)} %param.6) | copy-start | bytes 1572868

commit v7 on v6

--- a/solution.py
+++ b/solution.py
@@ -492,7 +492,8 @@
         send_back(sent.at[3], returned.at[3], 3)
 
     def send_tile(tile):
-        for upper in range(2):
+        for turn_of in range(2):
+            upper = lax.rem(core + turn_of, 2)
             other_core, other_y = tile // 2, 2 * (tile % 2) + upper
             mine = jnp.logical_and(core == other_core, y == other_y)
             source = rows.at[2, 2 * tile + upper]

time: 52.6 us -> 52.6 us (level)
  no operation moved by 1% of the time
where the time goes in v7:
time: 52.6 us; the launch traced here: 52.5 us
  Pallas kernels  51.6 us (98%)
  other arithmetic  0.92 us (2%)
    pallas_call x1, Pallas kernels, shards(): pl.pallas_call(kernel, out_shape=jax.ShapeDtypeStruct((count, channels),...  51.6 us

profile of v7, /device:TPU:1, one launch (start us, length us, event | category | flops | bytes accessed | tf_op | source)
XLA Modules:
  0.0 52.5 jit_solution(8828698976447159651)
XLA Ops:
  0.0 0.0 copy-start
  0.0 51.6 %shard_map.64 = bf16[64,4096]{1,0:T(8,128)(2,1)S(1)} custom-call(bf16[64,4096]{1,0:T(8,128)(2,1)} %key_hbm.1, bf16[64,4096]{1,0:T(8,128)(2,1)} %value_hbm.1, bf16[512,512]{1,0:T(8,128)(2,1)} %filter_hbm.1, f32[512]{0:T(512)} %gain_ref.1, f32[1024,256]{1,0:T(8,128)} %constant.2.clone.tables_hbm), custom_call_target="tpu_custom_call" | custom-call | tf_op jit(solution)/shard_map/pallas_call | solution.py:601
  51.6 0.0 copy-done
  51.6 0.9 %multiply_convert_fusion = bf16[64,4096]{1,0:T(8,128)(2,1)} fusion(bf16[64,4096]{1,0:T(8,128)(2,1)S(1)} %shard_map.64, bf16[64,4096]{1,0:T(8,128)(2,1)S(1)} %copy-done), kind=kLoop, calls=%fused_computation | loop fusion | flops 1048576 | bytes 1572864 | tf_op jit(solution)/shard_map/convert_element_type | solution.py:653
Async XLA Ops:
  0.0 51.6 %copy-start = (bf16[64,4096]{1,0:T(8,128)(2,1)S(1)}, bf16[64,4096]{1,0:T(8,128)(2,1)}, u32[]{:S(2)}) copy-start(bf16[64,4096]{1,0:T(8,128)(2,1)} %param.6) | copy-start | bytes 1572868
